TPU v7x, 768 devices: a whole 4x8x12 slice. The times are simulated.
768 devices in a mesh: row: 24 (over z_hi, y), col: 32 (over z_lo, x, core).
Axes of the slice: x: 4, y: 8, z: 12 (z_hi: 3, z_lo: 4; z = z_hi * 4 + z_lo), core: 2. Of those that a mesh axis runs over, the one named last changes fastest.
Arguments:
- iterate_tiles: bfloat16 [3072, 12288], P('row', 'col'), may hold values from -1.5 to 1.5
- tile_blocks: int32 [48, 96], P('row', 'col'), may hold values from -1 to 383, as said below
Outputs:
- next_tiles: bfloat16 [3072, 12288], P('row', 'col')
Inputs may be any that keep to these rules, and one draw needn't show every extreme that they name: `tile_blocks`: A used slot on process row p and process column q holds a block (I, J) with I mod (number of process rows) = p and (J + (J div number of process rows)) mod (number of process columns) = q, so a block's process column depends on its block column alone. No block appears twice, every diagonal block (I, I) appears, and unused slots hold -1 in both rows. At least one device uses all 3 slots; the order of slots within a device carries no meaning.
All inputs are finite; a program needn't handle non-finite values.
Results may differ from a plain program's by a relative error of at most 0.0048.
Values may be sent and summed in bfloat16 or wider, within the bound.
No kernel may reach another device: no remote copies, remote signals or barrier semaphores. Data moves between devices by JAX's collectives and lax.ppermute only.
A program may use at most 32 MiB of HBM per device.

v0:
```python
import jax
import jax.numpy as jnp
from jax import lax
from jax.sharding import PartitionSpec as P


def partner(fold_rows, fold_cols, keep_rows, keep_cols, out_rows, out_cols):
    folded_r = fold_rows[:, None, None]
    folded_c = fold_cols[:, None, None]
    kept_r = keep_rows[None, None, :]
    kept_c = keep_cols[None, None, :]
    target_r = out_rows[None, :, None]
    target_c = out_cols[None, :, None]
    linked = (folded_r == target_r) & (folded_c == kept_r) & (kept_c == target_c)
    linked = linked & (folded_r >= 0) & (kept_r >= 0) & (target_r >= 0)
    positions = jnp.arange(keep_rows.shape[0], dtype=jnp.int32)[None, None, :]
    partner_slot = jnp.sum(jnp.where(linked, positions, 0), axis=2)
    return (partner_slot, jnp.any(linked, axis=2))


def columns(tile_array, tile_blocks):
    return (
        lax.all_gather(tile_array, "row", axis=0, tiled=True),
        lax.all_gather(tile_blocks, "row", axis=0, tiled=True),
    )


def left_fold(left_tiles, tile_blocks, panel, panel_blocks):
    block_size = left_tiles.shape[0]
    slot_count = tile_blocks.shape[1]
    panel_rows = panel.shape[0] // block_size
    right_grid = panel.reshape(panel_rows, block_size, slot_count, block_size)
    kept_blocks = panel_blocks.reshape(panel_rows, 2, slot_count)
    kept_rows = kept_blocks[:, 0].reshape(-1)
    kept_cols = kept_blocks[:, 1].reshape(-1)
    piece_tiles = lax.all_gather(left_tiles, "col", axis=1, tiled=True)
    piece_blocks = lax.all_gather(tile_blocks, "col", axis=1, tiled=True)
    piece_slots = piece_blocks.shape[1]
    left_list = piece_tiles.reshape(block_size, piece_slots, block_size)
    partner_slot, matched = partner(
        piece_blocks[0], piece_blocks[1], kept_rows, kept_cols, tile_blocks[0], tile_blocks[1]
    )
    picked = right_grid[partner_slot // slot_count, :, partner_slot % slot_count, :]
    picked = picked * matched[:, :, None, None].astype(jnp.bfloat16)
    running = jnp.einsum("iak,aokj->ioj", left_list, picked, preferred_element_type=jnp.float32)
    return running.reshape(block_size, slot_count * block_size)


def per_device(iterate_tiles, tile_blocks):
    block_size = iterate_tiles.shape[0]
    slot_count = tile_blocks.shape[1]
    panel, panel_blocks = columns(iterate_tiles, tile_blocks)
    square = left_fold(iterate_tiles, tile_blocks, panel, panel_blocks).astype(jnp.bfloat16)
    panel, panel_blocks = columns(square, tile_blocks)
    cube = left_fold(iterate_tiles, tile_blocks, panel, panel_blocks)
    used = tile_blocks[0] >= 0
    updated = 1.5 * iterate_tiles.astype(jnp.float32) - 0.5 * cube
    shaped = updated.reshape(block_size, slot_count, block_size)
    kept = jnp.where(used[None, :, None], shaped, jnp.zeros_like(shaped))
    return kept.reshape(block_size, slot_count * block_size).astype(jnp.bfloat16)


def solution(mesh):
    return jax.shard_map(
        per_device,
        mesh=mesh,
        in_specs=(P("row", "col"), P("row", "col")),
        out_specs=P("row", "col"),
        check_vma=False,
    )
```

profile of v0, /device:TPU:6, one launch (start us, length us, event | category | flops | bytes accessed | tf_op | source)
XLA Modules:
  0.0 378.1 jit_solution(6343396852969195622)
XLA Ops:
  6.5 0.7 all-gather.6.cloned.1.call-update
  7.3 1.6 copy.42
  9.0 0.0 all-gather.10.cloned.1.call-start
  9.0 83.6 %all-gather.1 = s32[24,2,3]{2,1,0:T(2,128)S(1)} all-gather(s32[1,2,3]{2,1,0:T(2,128)} %bitcast.76), channel_id=1, replica_groups=mesh['row'=24,'col'=32] {'row'}, dimensions={0}, use_global_device_ids=true | all-gather | bytes 600 | tf_op jit(solution)/shard_map/all_gather | solution.py:24
  92.6 0.1 slice_reduce_fusion
  92.7 0.1 eq.97
  92.8 0.1 eq.94
  92.9 40.7 %all-gather = s32[32,3,2]{1,2,0:T(2,128)S(1)} all-gather(s32[1,3,2]{1,2,0:T(2,128)} %bitcast.77), channel_id=1, replica_groups=mesh['row'=24,'col'=32] {'col'}, dimensions={0}, use_global_device_ids=true | all-gather | bytes 792 | tf_op jit(solution)/shard_map/all_gather | solution.py:37
  133.6 0.1 reshape.243
  133.7 0.7 broadcast_compare_fusion.5
  134.4 0.8 slice_bitcast_fusion.3
  135.1 0.1 broadcast_compare_fusion.1
  135.2 0.1 broadcast_compare_fusion.2
  135.3 0.1 broadcast_compare_fusion
  135.4 0.1 fusion.26
  135.5 0.1 copy.41
  135.7 0.1 copy.39
  135.8 0.2 reshape.230
  136.0 0.8 all-gather.6.cloned.1.call-done
  136.8 7.0 %reshape.251 = bf16[24,128,3,128]{3,2,1,0:T(4,128)(2,1)} reshape(bf16[3072,384]{1,0:T(8,128)(2,1)} %all-gather.6.cloned.1.call-done) | data formatting | bytes 4718592 | tf_op jit(solution)/shard_map/reshape | solution.py:32
  143.9 2.6 copy.40
  146.4 18.9 %gather_fusion = bf16[288,128,128]{2,1,0:T(8,128)(2,1)} fusion(bf16[24,128,3,128]{3,1,2,0:T(8,128)(2,1)S(1)} %copy.40, s32[288]{0:T(512)S(1)} %reshape.230), kind=kCustom, calls=%fused_computation | custom fusion | bytes 18876672 | tf_op jit(solution)/shard_map/gather | solution.py:43
  165.3 40.1 %all-gather.8.cloned.1.call-done = bf16[128,12288]{0,1:T(8,128)(2,1)} async-done(((bf16[128,384]{0,1:T(8,128)(2,1)}), bf16[128,12288]{0,1:T(8,128)(2,1)}) %all-gather.8.cloned.1.call-update) | async-done | bytes 3145744 | tf_op jit(solution)/shard_map/all_gather | solution.py:36
  205.5 9.7 %fusion.15 = bf16[3,128,128]{2,1,0:T(8,128)(2,1)} fusion(bf16[128,96,128,1]{0,2,3,1:T(8,128)(2,1)} %bitcast.80, bf16[96,3,128,128]{3,2,1,0:T(8,128)(2,1)} %bitcast.70, bf16[96,3]{1,0:T(8,128)(2,1)S(1)} %copy.41), kind=kOutput, calls=%fused_computation.11 | convolution fusion | flops 1212727296 | bytes 12681792 | tf_op jit(solution)/shard_map/iak,aokj->ioj/dot_general | solution.py:45
  215.2 0.1 broadcast_bitcast_fusion
  215.3 120.2 %all-gather.10.cloned.1.call-done = bf16[3072,384]{0,1:T(8,128)(2,1)} async-done(((bf16[128,384]{0,1:T(8,128)(2,1)}), bf16[3072,384]{0,1:T(8,128)(2,1)}) %all-gather.10.cloned.1.call-update) | async-done | bytes 2359312 | tf_op jit(solution)/shard_map/all_gather | solution.py:23
  335.5 3.7 copy.59
  339.1 3.3 copy.45
  342.4 19.1 %gather_fusion.1 = bf16[288,128,128]{2,1,0:T(8,128)(2,1)} fusion(bf16[24,128,3,128]{3,1,2,0:T(8,128)(2,1)S(1)} %copy.45, s32[288]{0:T(512)S(1)} %reshape.230), kind=kCustom, calls=%fused_computation.1 | custom fusion | bytes 18876672 | tf_op jit(solution)/shard_map/gather | solution.py:43
  361.5 9.3 %fusion.12 = f32[3,128,128]{2,1,0:T(8,128)S(1)} fusion(bf16[128,96,128,1]{0,2,3,1:T(8,128)(2,1)} %bitcast.81, bf16[96,3,128,128]{3,2,1,0:T(8,128)(2,1)} %bitcast.71, bf16[96,3]{1,0:T(8,128)(2,1)S(1)} %copy.41), kind=kOutput, calls=%fused_computation.10 | convolution fusion | flops 1212727296 | bytes 12780096 | tf_op jit(solution)/shard_map/iak,aokj->ioj/dot_general | solution.py:45
  370.8 0.1 copy.48
  370.9 0.7 select_convert_fusion
  (13 shorter events, 0.2 us)
Async XLA Ops:
  6.5 130.3 %all-gather.6.cloned.1.call-start = ((), (), s32[]{:S(2)}) async-start(), calls=%async_computation | async-start | bytes 2457600 | tf_op jit(solution)/shard_map/all_gather | solution.py:23
  7.3 198.2 %all-gather.8.cloned.1.call-start = ((), (), s32[]{:S(2)}) async-start(), calls=%async_computation.1 | async-start | bytes 3244032 | tf_op jit(solution)/shard_map/all_gather | solution.py:36
  9.0 326.5 %all-gather.10.cloned.1.call-start = ((), (), s32[]{:S(2)}) async-start(), calls=%async_computation.2 | async-start | bytes 2457600 | tf_op jit(solution)/shard_map/all_gather | solution.py:23
  361.5 9.4 %copy-start = (bf16[128,384]{1,0:T(8,128)(2,1)S(1)}, bf16[128,384]{1,0:T(8,128)(2,1)}, u32[]{:S(2)}) copy-start(bf16[128,384]{1,0:T(8,128)(2,1)} %param.2) | copy-start | bytes 294916
Sparse Core Ops, SparseCore 0:
  11.4 125.4 all-gather.5
  139.3 66.1 all-gather.7
  215.3 120.0 all-gather.9
where the time goes:
time: 379 us; the launch traced here: 378 us
  waiting for transfers between devices  162 us (43%)
  blocking collectives  124 us (33%)
  local copies, waits for them, and re-layouts  57.9 us (15%)
  matrix products  19 us (5%)
  between operations  13.2 us (3%)
    all_gather x2, waiting for transfers between devices, columns(): lax.all_gather(tile_array, 'row', axis=0, tiled=True)  121 us
    all_gather x1, blocking collectives, columns(): lax.all_gather(tile_blocks, 'row', axis=0, tiled=True)  83.6 us
    all_gather x1, blocking collectives, left_fold(): piece_blocks = lax.all_gather(tile_blocks, 'col', axis=1, tiled=True)  40.7 us
    all_gather x1, waiting for transfers between devices, left_fold(): piece_tiles = lax.all_gather(left_tiles, 'col', axis=1, tiled=True)  40.1 us
    gather x2, local copies, waits for them, and re-layouts, left_fold(): right_grid[partner_slot // slot_count, :, partner_slot % slot_count, :]  38 us
    dot_general x2, matrix products, left_fold(): jnp.einsum('iak,aokj->ioj', left_list, picked, preferred_element_type=jnp...  19 us
    reshape x3, local copies, waits for them, and re-layouts, left_fold(): right_grid = panel.reshape(panel_rows, block_size, slot_count, block_size)  12.8 us
  transfers between devices with their start and end apart: 3, of which 3 were waited for; matrix products, arithmetic and copies ran while one was open for 9% of the time, Pallas kernels for 0%

commit v1 on v0

v1 whole, which is shorter than its diff:
```python
import jax
import jax.numpy as jnp
import numpy as np
from jax import lax
from jax.experimental import pallas as pl
from jax.experimental.pallas import tpu as pltpu
from jax.sharding import Mesh, PartitionSpec as P

BLK = 128
NB = 384
ZH, Y, ZL, X, C = 3, 8, 4, 4, 2
XC = X * C
N_ROW, N_COL = ZH * Y, ZL * XC
SLOTS = 3
TILES = SLOTS * BLK
HEAD = 16
FIRST = TILES + HEAD
COLPAD = 32
SECOND = TILES + COLPAD
ROW = ("zh", "y")
COL = ("zl", "x", "c")
F32 = jnp.float32
BF16 = jnp.bfloat16
PARAMS = pltpu.CompilerParams(vmem_limit_bytes=48 * 1024 * 1024)
VMEM = pl.BlockSpec(memory_space=pltpu.VMEM)
SMEM = pl.BlockSpec(memory_space=pltpu.SMEM)


def partner(fold_rows, fold_cols, keep_rows, keep_cols, out_rows, out_cols):
    folded_r = fold_rows[:, None, None]
    folded_c = fold_cols[:, None, None]
    kept_r = keep_rows[None, None, :]
    kept_c = keep_cols[None, None, :]
    target_r = out_rows[None, :, None]
    target_c = out_cols[None, :, None]
    linked = (folded_r == target_r) & (folded_c == kept_r) & (kept_c == target_c)
    linked = linked & (folded_r >= 0) & (kept_r >= 0) & (target_r >= 0)
    positions = jnp.arange(keep_rows.shape[0], dtype=jnp.int32)[None, None, :]
    partner_slot = jnp.sum(jnp.where(linked, positions, 0), axis=2)
    return (partner_slot, jnp.any(linked, axis=2))


def columns(tile_array, tile_blocks):
    return (
        lax.all_gather(tile_array, ROW, axis=0, tiled=True),
        lax.all_gather(tile_blocks, ROW, axis=0, tiled=True),
    )


def left_fold(left_tiles, tile_blocks, panel, panel_blocks):
    block_size = left_tiles.shape[0]
    slot_count = tile_blocks.shape[1]
    panel_rows = panel.shape[0] // block_size
    right_grid = panel.reshape(panel_rows, block_size, slot_count, block_size)
    kept_blocks = panel_blocks.reshape(panel_rows, 2, slot_count)
    kept_rows = kept_blocks[:, 0].reshape(-1)
    kept_cols = kept_blocks[:, 1].reshape(-1)
    piece_tiles = lax.all_gather(left_tiles, COL, axis=1, tiled=True)
    piece_blocks = lax.all_gather(tile_blocks, COL, axis=1, tiled=True)
    piece_slots = piece_blocks.shape[1]
    left_list = piece_tiles.reshape(block_size, piece_slots, block_size)
    partner_slot, matched = partner(
        piece_blocks[0], piece_blocks[1], kept_rows, kept_cols, tile_blocks[0], tile_blocks[1]
    )
    picked = right_grid[partner_slot // slot_count, :, partner_slot % slot_count, :]
    picked = picked * matched[:, :, None, None].astype(BF16)
    running = jnp.einsum("iak,aokj->ioj", left_list, picked, preferred_element_type=F32)
    return running.reshape(block_size, slot_count * block_size)


def general(iterate_tiles, tile_blocks):
    block_size = iterate_tiles.shape[0]
    slot_count = tile_blocks.shape[1]
    panel, panel_blocks = columns(iterate_tiles, tile_blocks)
    square = left_fold(iterate_tiles, tile_blocks, panel, panel_blocks).astype(BF16)
    panel, panel_blocks = columns(square, tile_blocks)
    cube = left_fold(iterate_tiles, tile_blocks, panel, panel_blocks)
    used = tile_blocks[0] >= 0
    updated = 1.5 * iterate_tiles.astype(F32) - 0.5 * cube
    shaped = updated.reshape(block_size, slot_count, block_size)
    kept = jnp.where(used[None, :, None], shaped, jnp.zeros_like(shaped))
    return kept.reshape(block_size, slot_count * block_size).astype(BF16)


def place():
    zh, y, zl = lax.axis_index("zh"), lax.axis_index("y"), lax.axis_index("zl")
    u = lax.axis_index("x") * C + lax.axis_index("c")
    return zh, y, zl, u, zh * Y + y, zl * XC + u


def iota(shape, dim):
    return lax.broadcasted_iota(jnp.int32, shape, dim)


def dot(a, b):
    return jnp.dot(a, b, preferred_element_type=F32)


def pack_kernel(blocks, x_ref, out_ref):
    u = place()[3]
    lane = iota((HEAD, 128), 1)
    head = jnp.zeros((HEAD, 128), F32)
    for s in range(SLOTS):
        for v in range(4):
            number = blocks[v // 2, s]
            part = (number >> 4) if v % 2 == 0 else (number & 15)
            head = jnp.where(lane == v * 32 + u * SLOTS + s, part.astype(F32), head)
    head = head.astype(BF16)
    for z in range(ZH):
        for s in range(SLOTS):
            out_ref[z, s * BLK : (s + 1) * BLK, :] = x_ref[:, s * BLK : (s + 1) * BLK]
        out_ref[z, TILES:, :] = head


def plan_kernel(
    blocks, g_ref, first_ref, second_ref, p_ref, qt_ref, q_ref, imod_ref, kmod_ref, own_ref, ownc_ref,
    ybuf_ref, zbuf_ref, list_ref,
    gij_ref, gt_ref, ohi_ref, ohj_ref, dy_ref, ry_ref, dl_ref, rl_ref, list_smem, sem,
):
    zh, y, zl, u, p, q = place()
    g = g_ref[...].reshape(ZL * COLPAD, 128).astype(F32)
    g = 16.0 * g + pltpu.roll(g, 96, 1)
    row128, lane128 = iota((128, 128), 0), iota((128, 128), 1)
    g = jnp.where(((row128 & 31) < N_ROW) & ((lane128 & 63) < XC * SLOTS), g, -1.0)
    gij_ref[...] = g
    gt = g.T
    gt_ref[...] = gt
    sub = iota((NB, 128), 0).astype(F32)
    wide = iota((128, NB), 1).astype(F32)

    def onehot(mask):
        return jnp.where(mask, 1.0, 0.0).astype(BF16)

    for k in range(XC * SLOTS):
        ohi_ref[:, k * 128 : (k + 1) * 128] = onehot(sub == gt[k : k + 1, :])
        ohj_ref[k * 128 : (k + 1) * 128, :] = onehot(wide == g[:, 64 + k : 65 + k])
    adj = dot(ohi_ref[...], ohj_ref[...])
    adj_b = adj.astype(BF16)
    adj_t = adj.T.astype(BF16)
    lane = iota((1, 128), 1)
    rows = iota((32, 128), 0)
    lanes = iota((32, 128), 1)

    ci = jnp.full((1, 128), -1.0, F32)
    cj = jnp.full((1, 128), -1.0, F32)
    for s in range(SLOTS):
        shift = (s * 32 + 128 - zl * 32) & 127
        here = (lane >> 5 == s) & ((lane & 31) < N_ROW)
        rows_i = jnp.broadcast_to(gt_ref[pl.ds(u * SLOTS + s, 1), :], (8, 128))
        rows_j = jnp.broadcast_to(gt_ref[pl.ds(64 + u * SLOTS + s, 1), :], (8, 128))
        ci = jnp.where(here, pltpu.roll(rows_i, shift, 1)[0:1], ci)
        cj = jnp.where(here, pltpu.roll(rows_j, shift, 1)[0:1], cj)
    both = dot(adj_b, onehot(sub == cj)) * dot(adj_b, onehot(sub == ci))
    wanted = (dot(p_ref[...], both.astype(BF16)) > 0.5) & ((lanes & 31) != rows)
    wanted = jnp.where(wanted, 1.0, 0.0)
    dy_ref[...] = wanted
    ry_ref[...] = dot(wanted.astype(BF16), onehot((row128 < lane128) & ((row128 & 7) == (lane128 & 7))))

    li = jnp.full((1, 128), -1.0, F32)
    lk = jnp.full((1, 128), -1.0, F32)
    for z in range(ZL):
        here = (lane >> 5 == z) & ((lane & 31) < XC * SLOTS)
        mine = jnp.broadcast_to(gij_ref[pl.ds(z * COLPAD + p, 1), :], (8, 128))
        li = jnp.where(here, (pltpu.roll(mine, z * 32, 1) if z else mine)[0:1], li)
        lk = jnp.where(here, pltpu.roll(mine, (64 + z * 32) % 128, 1)[0:1], lk)
    both = dot(adj_t, onehot(sub == li)) * dot(adj_t, onehot(sub == lk))
    owner = (lanes >> 5) * XC + (((lanes & 31) * 11) >> 5)
    wanted = (dot(qt_ref[...], both.astype(BF16)) > 0.5) & (owner != rows) & ((lanes & 31) < XC * SLOTS)
    wanted = jnp.where(wanted, 1.0, 0.0)
    dl_ref[...] = wanted
    rl_ref[...] = dot(wanted.astype(BF16), onehot((row128 < lane128) & ((row128 >> 5) == (lane128 >> 5))))

    lanes8 = iota((8, 128), 1)
    rows8 = iota((8, 128), 0)
    send_d = dy_ref[pl.ds(pl.multiple_of(zh * Y, 8), 8), :]
    send_r = ry_ref[pl.ds(pl.multiple_of(zh * Y, 8), 8), :]
    ylist = jnp.zeros((8, 128), F32)
    for c in range(SLOTS):
        hit = (send_d > 0.5) & (send_r == float(c)) & ((lanes8 & 7) == y)
        code = jnp.sum(jnp.where(hit, (lanes8 + 1).astype(F32), 0.0), axis=1, keepdims=True)
        ylist = jnp.where(lanes8 == c, code, ylist)
    send_d = jnp.zeros((8, 128), F32)
    send_r = jnp.zeros((8, 128), F32)
    for z in range(ZL):
        send_d = jnp.where(rows8 == z, dl_ref[pl.ds(z * XC + u, 1), :], send_d)
        send_r = jnp.where(rows8 == z, rl_ref[pl.ds(z * XC + u, 1), :], send_r)
    zlist = jnp.zeros((8, 128), F32)
    for c in range(SLOTS):
        hit = (send_d > 0.5) & (send_r == float(c)) & ((lanes8 >> 5) == zl)
        code = jnp.sum(jnp.where(hit, ((lanes8 & 31) + 1).astype(F32), 0.0), axis=1, keepdims=True)
        zlist = jnp.where(lanes8 == c, code, zlist)

    got_d, got_r = dy_ref[pl.ds(p, 1), :], ry_ref[pl.ds(p, 1), :]
    right = jnp.where(got_d > 0.5, ((lane & 7) * SLOTS + 1).astype(F32) + got_r, 0.0)
    right = jnp.where(((lane & 31) == p) & (ci >= 0.0), (Y * SLOTS + 1 + (lane >> 5)).astype(F32), right)
    stack = jnp.where(row128 == 0, ci, jnp.where(row128 == 1, cj, right)).T
    ci_c, cj_c, right_c = stack[:, 0:1], stack[:, 1:2], stack[:, 2:3]
    linked = jnp.where(ci_c == lk, right_c, 0.0)
    meets = jnp.zeros((8, 128), F32)
    for o in range(SLOTS):
        out_i, out_j = blocks[0, o].astype(F32), blocks[1, o].astype(F32)
        met = jnp.sum(jnp.where(cj_c == out_j, linked, 0.0), axis=0, keepdims=True)
        met = jnp.where(li == out_i, met, 0.0)
        meets = jnp.where(rows8 == o, met, meets)
    got_d, got_r = dl_ref[pl.ds(q, 1), :], rl_ref[pl.ds(q, 1), :]
    terms = jnp.zeros((8, 128), F32)
    for t in range(ZL * SLOTS + SLOTS):
        if t < ZL * SLOTS:
            hit = (lane >> 5 == t // SLOTS) & (got_d > 0.5) & (got_r == float(t % SLOTS))
        else:
            hit = lane == zl * 32 + u * SLOTS + (t - ZL * SLOTS)
        value = jnp.sum(jnp.where(hit, meets, 0.0), axis=1, keepdims=True)
        terms = jnp.where(lanes8 == t, value, terms)

    most = jnp.zeros((32, 32), F32)
    from_row = jnp.where(imod_ref[...] != kmod_ref[...], adj, 0.0)
    to_col = jnp.where(ownc_ref[...] != own_ref[...], adj, 0.0).astype(BF16)
    k_lane = iota((NB, NB), 1)
    own_lane = own_ref[...] >> 3
    for c in range(Y + ZL):
        if c < Y:
            count = dot(jnp.where((k_lane & 7) == c, from_row, 0.0).astype(BF16), adj_b)
        else:
            count = dot(jnp.where(own_lane == c - Y, adj, 0.0).astype(BF16), to_col)
        count = (count * adj).astype(BF16)
        per_row = dot(p_ref[...], count)
        most = jnp.maximum(most, dot(per_row.astype(BF16), q_ref[...]))
    over = jnp.where(jnp.max(most, keepdims=True).reshape(1, 1) > SLOTS + 0.5, 1.0, 0.0)
    zlist = jnp.where((rows8 == 7) & (lanes8 == 0), over, zlist)

    list_ref[0:8, :] = ylist.astype(jnp.int32)
    list_ref[8:16, :] = zlist.astype(jnp.int32)
    list_ref[16:24, :] = terms.astype(jnp.int32)
    copy = pltpu.make_async_copy(list_ref, list_smem, sem)
    copy.start()
    copy.wait()
    pick_y(list_smem, first_ref, FIRST, ybuf_ref)
    for d in range(ZL):
        for c in range(SLOTS):
            code = list_smem[8 + d, c]

            @pl.when(code > 0)
            def _():
                k = code - 1
                src_u = (k * 11) >> 5
                start = pl.multiple_of(src_u * SECOND + (k - src_u * SLOTS) * BLK, 16)
                zbuf_ref[d, c * BLK : (c + 1) * BLK, :] = second_ref[pl.ds(start, BLK), :]


def pick_y(lists, src_ref, stride, ybuf_ref):
    for d in range(Y):
        for c in range(SLOTS):
            code = lists[d, c]

            @pl.when(code > 0)
            def _():
                r = code - 1
                start = pl.multiple_of(((r >> 3) & 3) * stride + (r >> 5) * BLK, 16)
                ybuf_ref[d, c * BLK : (c + 1) * BLK, :] = src_ref[pl.ds(start, BLK), :]


def pick_kernel(lists, src_ref, ybuf_ref):
    pick_y(lists, src_ref, TILES, ybuf_ref)


def accumulate(lists, o, acc_ref, x_ref, left_ref, own_right, right_ref):
    acc_ref[...] = jnp.zeros((BLK, BLK), F32)
    for t in range(ZL * SLOTS + SLOTS):
        code = lists[16 + o, t]
        if t < ZL * SLOTS:
            left = left_ref.at[t * BLK : (t + 1) * BLK, :]
        else:
            left = x_ref.at[:, (t - ZL * SLOTS) * BLK : (t - ZL * SLOTS + 1) * BLK]

        @pl.when((code > 0) & (code <= Y * SLOTS))
        def _():
            start = pl.multiple_of((code - 1) * BLK, BLK)
            acc_ref[...] += dot(left[...], right_ref[pl.ds(start, BLK), :])

        @pl.when(code > Y * SLOTS)
        def _():
            start = pl.multiple_of((code - 1 - Y * SLOTS) * BLK, BLK)
            acc_ref[...] += dot(left[...], own_right[pl.ds(start, BLK), :])


def square_kernel(lists, x_ref, own_ref, left_ref, right_ref, out_ref, acc_ref):
    for o in range(SLOTS):
        accumulate(lists, o, acc_ref, x_ref, left_ref, own_ref, right_ref)
        tile = acc_ref[...].astype(BF16)
        for z in range(ZH):
            out_ref[z, o * BLK : (o + 1) * BLK, :] = tile


def cube_kernel(lists, blocks, x_ref, own_ref, left_ref, right_ref, out_ref, acc_ref):
    for o in range(SLOTS):
        accumulate(lists, o, acc_ref, x_ref, left_ref, own_ref, right_ref)
        part = slice(o * BLK, (o + 1) * BLK)
        value = 1.5 * x_ref[:, part].astype(F32) - 0.5 * acc_ref[...]
        out_ref[:, part] = jnp.where(blocks[0, o] >= 0, value, 0.0).astype(BF16)


def swap(value, axes):
    return lax.all_to_all(value, axes, 0, 0, tiled=True)


def tables():
    number = np.arange(NB)
    owner = (number + number // N_ROW) % N_COL
    in_row = (number[None, :] % N_ROW == np.arange(32)[:, None]).astype(jnp.bfloat16)
    in_col = (owner[None, :] == np.arange(32)[:, None]).astype(jnp.bfloat16)
    mod = (number % N_ROW).astype(np.int32)
    owner = owner.astype(np.int32)
    return (
        in_row, in_col, np.ascontiguousarray(in_col.T),
        mod[:, None], mod[None, :], owner[None, :], owner[:, None],
    )


def per_device(x, blocks):
    first = pl.pallas_call(
        pack_kernel,
        out_shape=jax.ShapeDtypeStruct((ZH, FIRST, BLK), BF16),
        in_specs=[SMEM, VMEM], out_specs=VMEM, compiler_params=PARAMS, name="pack",
    )(blocks, x)
    own = first[0, :TILES]
    first = swap(first, "zh")
    heads = jnp.pad(first[:, TILES], ((0, HEAD - ZH), (0, 0)))
    heads = swap(jnp.broadcast_to(heads[None], (Y, HEAD, 128)).reshape(Y * HEAD, 128), "y")
    heads = heads.reshape(Y, HEAD, 128)[:, :ZH].transpose(1, 0, 2).reshape(N_ROW, 128)
    heads = jnp.pad(heads, ((0, COLPAD - N_ROW), (0, 0)))
    second = lax.all_gather(jnp.concatenate([own, heads], axis=0), ("x", "c"), axis=0)
    heads = jnp.sum(second[:, TILES:].astype(F32), axis=0).astype(BF16)
    heads = swap(jnp.broadcast_to(heads[None], (ZL, COLPAD, 128)).reshape(ZL * COLPAD, 128), "zl")
    ybuf, zbuf, lists = pl.pallas_call(
        plan_kernel,
        out_shape=(
            jax.ShapeDtypeStruct((Y, TILES, BLK), BF16),
            jax.ShapeDtypeStruct((ZL, TILES, BLK), BF16),
            jax.ShapeDtypeStruct((24, 128), jnp.int32),
        ),
        in_specs=[SMEM] + [VMEM] * 10, out_specs=(VMEM,) * 3,
        scratch_shapes=[
            pltpu.VMEM((128, 128), F32), pltpu.VMEM((128, 128), F32),
            pltpu.VMEM((NB, XC * SLOTS * 128), BF16), pltpu.VMEM((XC * SLOTS * 128, NB), BF16),
            pltpu.VMEM((32, 128), F32), pltpu.VMEM((32, 128), F32),
            pltpu.VMEM((32, 128), F32), pltpu.VMEM((32, 128), F32),
            pltpu.SMEM((24, 128), jnp.int32), pltpu.SemaphoreType.DMA,
        ],
        compiler_params=PARAMS, name="plan",
    )(
        blocks, heads.reshape(ZL, COLPAD, 128), first.reshape(ZH * FIRST, BLK),
        second.reshape(XC * SECOND, BLK), *[jnp.asarray(t) for t in tables()],
    )
    left = swap(zbuf, "zl").reshape(ZL * TILES, BLK)
    right = swap(ybuf, "y").reshape(Y * TILES, BLK)
    square = pl.pallas_call(
        square_kernel,
        out_shape=jax.ShapeDtypeStruct((ZH, TILES, BLK), BF16),
        in_specs=[SMEM] + [VMEM] * 4, out_specs=VMEM,
        scratch_shapes=[pltpu.VMEM((BLK, BLK), F32)], compiler_params=PARAMS, name="square",
    )(lists, x, own, left, right)
    own_square = square[0]
    square = swap(square, "zh")
    ybuf = pl.pallas_call(
        pick_kernel,
        out_shape=jax.ShapeDtypeStruct((Y, TILES, BLK), BF16),
        in_specs=[SMEM, VMEM], out_specs=VMEM, compiler_params=PARAMS, name="pick",
    )(lists, square.reshape(ZH * TILES, BLK))
    right = swap(ybuf, "y").reshape(Y * TILES, BLK)
    result = pl.pallas_call(
        cube_kernel,
        out_shape=jax.ShapeDtypeStruct(x.shape, BF16),
        in_specs=[SMEM, SMEM] + [VMEM] * 4, out_specs=VMEM,
        scratch_shapes=[pltpu.VMEM((BLK, BLK), F32)], compiler_params=PARAMS, name="cube",
    )(lists, blocks, x, own_square, left, right)
    return lax.cond(lists[15, 0] > 0, lambda: general(x, blocks), lambda: result)


def solution(mesh):
    fine = Mesh(mesh.devices.reshape(ZH, Y, ZL, X, C), ROW + COL)
    return jax.shard_map(
        per_device,
        mesh=fine,
        in_specs=(P(ROW, COL), P(ROW, COL)),
        out_specs=P(ROW, COL),
        check_vma=False,
    )
```

time: 379 us -> 184 us (0.49)
  waiting for transfers between devices: 162 us -> 28.5 us
  local copies, waits for them, and re-layouts: 57.9 us -> 7.41 us
  matrix products: 19 us -> 0 us
  blocking collectives: 124 us -> 106 us
  Pallas kernels: 0 us -> 16.3 us
  starting transfers between devices: 0.08 us -> 10.6 us
    all_gather x3 -> x0, waiting for transfers between devices: 161 us -> none  [the longest x2 121 us: columns(): lax.all_gather(tile_array, 'row', axis=0, tiled=True)]
    all_gather x2 -> x1, blocking collectives: 124 us -> 13.6 us  [per_device(): lax.all_gather(jnp.concatenate([own, heads], axis=0), ('x', 'c'), axis=0)]
    all_to_all x0 -> x5, blocking collectives: none -> 92.5 us  [swap(): return lax.all_to_all(value, axes, 0, 0, tiled=True)]
    gather x2 -> x0, local copies, waits for them, and re-layouts: 38 us -> none  [left_fold(): right_grid[partner_slot // slot_count, :, partner_slot % slot_count, :]]
    all_to_all x0 -> x2, waiting for transfers between devices: none -> 28.5 us  [swap(): return lax.all_to_all(value, axes, 0, 0, tiled=True)]
    dot_general x2 -> x0, matrix products: 19 us -> none  [left_fold(): jnp.einsum('iak,aokj->ioj', left_list, picked, preferred_element_type=jnp...]
    pallas_call x0 -> x5, Pallas kernels: none -> 16.3 us  [the longest x1 10.2 us: per_device(): pl.pallas_call(plan_kernel, out_shape=(jax.ShapeDtypeStruct((Y, TILES, BL...]
    reshape x3 -> x0, local copies, waits for them, and re-layouts: 12.8 us -> none  [left_fold(): right_grid = panel.reshape(panel_rows, block_size, slot_count, block_size)]
  transfers between devices with their start and end apart: 3 -> 2, of which waited for: 3 -> 2; matrix products, arithmetic and copies ran while one was open for 9% -> 0% of each run, Pallas kernels for 0% -> 0%
where the time goes in v1:
time: 184 us; the launch traced here: 183 us
  blocking collectives  106 us (58%)
  waiting for transfers between devices  28.5 us (15%)
  Pallas kernels  16.3 us (9%)
  between operations  14.1 us (8%)
  starting transfers between devices  10.6 us (6%)
  local copies, waits for them, and re-layouts  7.41 us (4%)
    all_to_all x5, blocking collectives, swap(): return lax.all_to_all(value, axes, 0, 0, tiled=True)  92.5 us
    all_to_all x2, waiting for transfers between devices, swap(): return lax.all_to_all(value, axes, 0, 0, tiled=True)  28.5 us
    all_gather x1, blocking collectives, per_device(): lax.all_gather(jnp.concatenate([own, heads], axis=0), ('x', 'c'), axis=0)  13.6 us
    all_to_all x2, starting transfers between devices, swap(): return lax.all_to_all(value, axes, 0, 0, tiled=True)  10.6 us
    pallas_call x1, Pallas kernels, per_device(): pl.pallas_call(plan_kernel, out_shape=(jax.ShapeDtypeStruct((Y, TILES, BL...  10.2 us
    unnamed x21, local copies, waits for them, and re-layouts  6.23 us
  transfers between devices with their start and end apart: 2, of which 2 were waited for; matrix products, arithmetic and copies ran while one was open for 0% of the time, Pallas kernels for 0%

profile of v1, /device:TPU:6, one launch (start us, length us, event | category | flops | bytes accessed | tf_op | source)
XLA Modules:
  0.0 183.1 jit_solution(13732979551374437487)
XLA Ops:
  6.5 0.0 copy-start.10
  6.5 0.0 copy-start.7
  6.5 1.0 pack.1
  7.6 27.9 %all_to_all.37 = bf16[3,400,128]{2,1,0:T(8,128)(2,1)S(1)} all-to-all(bf16[3,400,128]{2,1,0:T(8,128)(2,1)S(1)} %pack.1), channel_id=1, replica_groups=mesh['zh'=3,'y'=8,'zl'=4,'x'=4,'c'=2] {'zh'}, dimensions={0} | all-to-all | bytes 614400 | tf_op jit(solution)/shard_map/all_to_all | solution.py:303
  35.5 0.6 broadcast_in_dim.49
  36.1 7.1 %all-to-all-start.1 = ((bf16[8,16,128]{2,1,0:T(8,128)(2,1)}), bf16[8,16,128]{2,1,0:T(8,128)(2,1)S(1)}, u32[]{:S(2)}, u32[]{:S(2)}) async-start(bf16[8,16,128]{2,1,0:T(8,128)(2,1)} %broadcast_in_dim.49), calls=%async_computation.1 | async-start | bytes 65536 | tf_op jit(solution)/shard_map/all_to_all | solution.py:303
  43.2 8.0 %all-to-all-done.1 = bf16[8,16,128]{2,1,0:T(8,128)(2,1)S(1)} async-done(((bf16[8,16,128]{2,1,0:T(8,128)(2,1)}), bf16[8,16,128]{2,1,0:T(8,128)(2,1)S(1)}, u32[]{:S(2)}, u32[]{:S(2)}) %all-to-all-start.1) | async-done | bytes 32800 | tf_op jit(solution)/shard_map/all_to_all | solution.py:303
  51.2 13.6 %all-gather.second_ref = bf16[3328,128]{1,0:T(8,128)(2,1)S(1)} all-gather(bf16[416,128]{1,0:T(8,128)(2,1)S(1)} %fusion.29), channel_id=2, replica_groups=mesh['zh'=3,'y'=8,'zl'=4,'x'=4,'c'=2] {'x','c'}, dimensions={0}, use_global_device_ids=true | all-gather | bytes 958464 | tf_op jit(solution)/shard_map/all_gather | solution.py:331
  64.9 10.9 %all_to_all.38.g_ref = bf16[4,32,128]{2,1,0:T(8,128)(2,1)S(1)} all-to-all(bf16[4,32,128]{2,1,0:T(8,128)(2,1)S(1)} %broadcast_in_dim.50), channel_id=1, replica_groups=mesh['zh'=3,'y'=8,'zl'=4,'x'=4,'c'=2] {'zl'}, dimensions={0} | all-to-all | bytes 65536 | tf_op jit(solution)/shard_map/all_to_all | solution.py:303
  75.7 0.0 copy-start
  75.7 0.9 copy-done
  76.7 0.0 copy-start.1
  76.7 0.9 copy-done.1
  77.6 0.9 copy-done.2
  78.5 0.7 copy-done.3
  79.2 0.7 copy-done.4
  80.0 0.7 copy-done.5
  80.6 0.7 copy-done.6
  81.3 10.2 %plan.1 = (bf16[8,384,128]{2,1,0:T(8,128)(2,1)S(1)}, bf16[4,384,128]{2,1,0:T(8,128)(2,1)S(1)}, s32[24,128]{1,0:T(8,128)S(1)}) custom-call(s32[2,3]{1,0:T(2,128)} %blocks.5, bf16[4,32,128]{2,1,0:T(8,128)(2,1)S(1)} %all_to_all.38.g_ref, bf16[1200,128]{1,0:T(8,128)(2,1)S(1)} %bitcast.104, bf16[3328,128]{1,0:T(8,128)(2,1)S(1)} %all-gather.second_ref, ...), custom_call_target="tpu_custom_call" | custom-call | tf_op jit(solution)/shard_map/plan/pallas_call | solution.py:334
  91.5 13.4 %all_to_all.39 = bf16[4,384,128]{2,1,0:T(8,128)(2,1)S(1)} all-to-all(bf16[4,384,128]{2,1,0:T(8,128)(2,1)S(1)} %get-tuple-element.19), channel_id=1, replica_groups=mesh['zh'=3,'y'=8,'zl'=4,'x'=4,'c'=2] {'zl'}, dimensions={0} | all-to-all | bytes 786432 | tf_op jit(solution)/shard_map/all_to_all | solution.py:303
  104.9 24.2 %all_to_all.40 = bf16[8,384,128]{2,1,0:T(8,128)(2,1)S(1)} all-to-all(bf16[8,384,128]{2,1,0:T(8,128)(2,1)S(1)} %get-tuple-element.20), channel_id=1, replica_groups=mesh['zh'=3,'y'=8,'zl'=4,'x'=4,'c'=2] {'y'}, dimensions={0} | all-to-all | bytes 1572864 | tf_op jit(solution)/shard_map/all_to_all | solution.py:303
  129.2 1.6 square.1
  130.8 16.0 %all_to_all.41 = bf16[3,384,128]{2,1,0:T(8,128)(2,1)S(1)} all-to-all(bf16[3,384,128]{2,1,0:T(8,128)(2,1)S(1)} %square.1), channel_id=1, replica_groups=mesh['zh'=3,'y'=8,'zl'=4,'x'=4,'c'=2] {'zh'}, dimensions={0} | all-to-all | bytes 589824 | tf_op jit(solution)/shard_map/all_to_all | solution.py:303
  146.8 1.8 %pick.1 = bf16[8,384,128]{2,1,0:T(8,128)(2,1)} custom-call(s32[24,128]{1,0:T(8,128)S(1)} %get-tuple-element.18.lists, bf16[1152,128]{1,0:T(8,128)(2,1)S(1)} %bitcast.105), custom_call_target="tpu_custom_call" | custom-call | tf_op jit(solution)/shard_map/pick/pallas_call | solution.py:364
  148.7 3.5 %all-to-all-start.6 = ((bf16[8,384,128]{2,1,0:T(8,128)(2,1)}), bf16[8,384,128]{2,1,0:T(8,128)(2,1)S(1)}, u32[]{:S(2)}, u32[]{:S(2)}) async-start(bf16[8,384,128]{2,1,0:T(8,128)(2,1)} %pick.1), calls=%async_computation.6 | async-start | bytes 1572864 | tf_op jit(solution)/shard_map/all_to_all | solution.py:303
  152.2 0.5 slice.47
  153.4 20.5 %all-to-all-done.6 = bf16[8,384,128]{2,1,0:T(8,128)(2,1)S(1)} async-done(((bf16[8,384,128]{2,1,0:T(8,128)(2,1)}), bf16[8,384,128]{2,1,0:T(8,128)(2,1)S(1)}, u32[]{:S(2)}, u32[]{:S(2)}) %all-to-all-start.6) | async-done | bytes 786464 | tf_op jit(solution)/shard_map/all_to_all | solution.py:303
  173.9 0.0 copy-done.10
  173.9 0.0 copy-done.7
  173.9 1.7 cube.1
  175.6 0.0 copy-start.9
  175.6 0.6 copy-done.9
  (16 shorter events, 0.1 us)
Async XLA Ops:
  6.5 167.3 %copy-start.10 = (s32[2,3]{1,0:T(2,128)S(1)}, s32[2,3]{1,0:T(2,128)}, u32[]{:S(2)}) copy-start(s32[2,3]{1,0:T(2,128)} %blocks.5) | copy-start | bytes 76
  6.5 167.3 %copy-start.7 = (bf16[128,384]{1,0:T(8,128)(2,1)S(1)}, bf16[128,384]{1,0:T(8,128)(2,1)}, u32[]{:S(2)}) copy-start(bf16[128,384]{1,0:T(8,128)(2,1)} %x_ref.5) | copy-start | bytes 294916
  36.1 15.1 %all-to-all-start.1 = ((bf16[8,16,128]{2,1,0:T(8,128)(2,1)}), bf16[8,16,128]{2,1,0:T(8,128)(2,1)S(1)}, u32[]{:S(2)}, u32[]{:S(2)}) async-start(bf16[8,16,128]{2,1,0:T(8,128)(2,1)} %broadcast_in_dim.49), calls=%async_computation.1 | async-start | bytes 65536 | tf_op jit(solution)/shard_map/all_to_all | solution.py:303
  75.7 0.9 copy-start
  76.7 0.9 copy-start.1
  77.6 0.9 copy-start.2
  78.5 0.7 copy-start.3
  79.2 0.7 copy-start.4
  79.9 0.7 copy-start.5
  80.6 0.7 copy-start.6
  148.7 25.2 %all-to-all-start.6 = ((bf16[8,384,128]{2,1,0:T(8,128)(2,1)}), bf16[8,384,128]{2,1,0:T(8,128)(2,1)S(1)}, u32[]{:S(2)}, u32[]{:S(2)}) async-start(bf16[8,384,128]{2,1,0:T(8,128)(2,1)} %pick.1), calls=%async_computation.6 | async-start | bytes 1572864 | tf_op jit(solution)/shard_map/all_to_all | solution.py:303
  175.6 0.6 copy-start.9

commit v2 on v0

v2 whole, which is shorter than its diff:
```python
import jax
import jax.numpy as jnp
from jax import lax
from jax.experimental import pallas as pl
from jax.experimental.pallas import tpu as pltpu
from jax.sharding import Mesh, PartitionSpec as P

BLK = 128
NB = 384
ZH, Y, ZL, X, C = 3, 8, 4, 4, 2
XC = X * C
N_ROW, N_COL = ZH * Y, ZL * XC
SLOTS = 3
TILES = SLOTS * BLK
HEAD = 32
PANEL = TILES + HEAD
SLOTS_ROW = XC * SLOTS
LEFTS = ZL * SLOTS + SLOTS
OWN, PLAIN = 128, 160
ZLIST, TERMS = 32, 40
ROW = ("zh", "y")
COL = ("zl", "x", "c")
F32 = jnp.float32
BF16 = jnp.bfloat16
PARAMS = pltpu.CompilerParams(vmem_limit_bytes=48 * 1024 * 1024)
VMEM = pl.BlockSpec(memory_space=pltpu.VMEM)
SMEM = pl.BlockSpec(memory_space=pltpu.SMEM)


def partner(fold_rows, fold_cols, keep_rows, keep_cols, out_rows, out_cols):
    folded_r = fold_rows[:, None, None]
    folded_c = fold_cols[:, None, None]
    kept_r = keep_rows[None, None, :]
    kept_c = keep_cols[None, None, :]
    target_r = out_rows[None, :, None]
    target_c = out_cols[None, :, None]
    linked = (folded_r == target_r) & (folded_c == kept_r) & (kept_c == target_c)
    linked = linked & (folded_r >= 0) & (kept_r >= 0) & (target_r >= 0)
    positions = jnp.arange(keep_rows.shape[0], dtype=jnp.int32)[None, None, :]
    partner_slot = jnp.sum(jnp.where(linked, positions, 0), axis=2)
    return (partner_slot, jnp.any(linked, axis=2))


def columns(tile_array, tile_blocks):
    return (
        lax.all_gather(tile_array, ROW, axis=0, tiled=True),
        lax.all_gather(tile_blocks, ROW, axis=0, tiled=True),
    )


def left_fold(left_tiles, tile_blocks, panel, panel_blocks):
    block_size = left_tiles.shape[0]
    slot_count = tile_blocks.shape[1]
    panel_rows = panel.shape[0] // block_size
    right_grid = panel.reshape(panel_rows, block_size, slot_count, block_size)
    kept_blocks = panel_blocks.reshape(panel_rows, 2, slot_count)
    kept_rows = kept_blocks[:, 0].reshape(-1)
    kept_cols = kept_blocks[:, 1].reshape(-1)
    piece_tiles = lax.all_gather(left_tiles, COL, axis=1, tiled=True)
    piece_blocks = lax.all_gather(tile_blocks, COL, axis=1, tiled=True)
    piece_slots = piece_blocks.shape[1]
    left_list = piece_tiles.reshape(block_size, piece_slots, block_size)
    partner_slot, matched = partner(
        piece_blocks[0], piece_blocks[1], kept_rows, kept_cols, tile_blocks[0], tile_blocks[1]
    )
    picked = right_grid[partner_slot // slot_count, :, partner_slot % slot_count, :]
    picked = picked * matched[:, :, None, None].astype(BF16)
    running = jnp.einsum("iak,aokj->ioj", left_list, picked, preferred_element_type=F32)
    return running.reshape(block_size, slot_count * block_size)


def general(iterate_tiles, tile_blocks):
    block_size = iterate_tiles.shape[0]
    slot_count = tile_blocks.shape[1]
    panel, panel_blocks = columns(iterate_tiles, tile_blocks)
    square = left_fold(iterate_tiles, tile_blocks, panel, panel_blocks).astype(BF16)
    panel, panel_blocks = columns(square, tile_blocks)
    cube = left_fold(iterate_tiles, tile_blocks, panel, panel_blocks)
    used = tile_blocks[0] >= 0
    updated = 1.5 * iterate_tiles.astype(F32) - 0.5 * cube
    shaped = updated.reshape(block_size, slot_count, block_size)
    kept = jnp.where(used[None, :, None], shaped, jnp.zeros_like(shaped))
    return kept.reshape(block_size, slot_count * block_size).astype(BF16)


def place():
    zh, y, zl = lax.axis_index("zh"), lax.axis_index("y"), lax.axis_index("zl")
    u = lax.axis_index("x") * C + lax.axis_index("c")
    return zh, y, zl, u, zh * Y + y, zl * XC + u


def iota(shape, dim):
    return lax.broadcasted_iota(jnp.int32, shape, dim)


def dot(a, b):
    return jnp.dot(a, b, preferred_element_type=F32)


def onehot(mask):
    return jnp.where(mask, 1.0, 0.0).astype(BF16)


def row_of(number):
    return number - N_ROW * ((number * 683) >> 14)


def col_of(number):
    return (number + ((number * 683) >> 14)) & (N_COL - 1)


def pack_kernel(blocks, x_ref, out_ref, own_ref):
    zh, y, zl, u, p, q = place()
    lane = iota((HEAD, 128), 1)
    here = iota((HEAD, 128), 0) == p
    head = jnp.zeros((HEAD, 128), F32)
    for s in range(SLOTS):
        for v in range(4):
            number = blocks[v // 2, s]
            part = (number >> 4) if v % 2 == 0 else (number & 15)
            head = jnp.where(here & (lane == v * 32 + u * SLOTS + s), part.astype(F32), head)
    head = head.astype(BF16)
    for s in range(SLOTS):
        tile = x_ref[:, s * BLK : (s + 1) * BLK]
        own_ref[s * BLK : (s + 1) * BLK, :] = tile
        for z in range(ZH):
            out_ref[z, s * BLK : (s + 1) * BLK, :] = tile
    for z in range(ZH):
        out_ref[z, TILES:, :] = head


def plan_kernel(
    blocks, g_ref, second_ref, zbuf_ref, list_ref,
    gij_ref, gt_ref, ohi_ref, ohj_ref, dl_ref, rl_ref, list_smem, sem,
):
    zh, y, zl, u, p, q = place()
    g = jnp.sum(g_ref[...].astype(F32), axis=0)
    g = 16.0 * g + pltpu.roll(g, 96, 1)
    row128, lane128 = iota((128, 128), 0), iota((128, 128), 1)
    g = jnp.where(((row128 & 31) < N_ROW) & ((lane128 & 63) < SLOTS_ROW), g, -1.0)
    gij_ref[...] = g
    gt = g.T
    gt_ref[...] = gt
    sub = iota((NB, 128), 0).astype(F32)
    wide = iota((128, NB), 1).astype(F32)
    for k in range(SLOTS_ROW):
        ohi_ref[:, k * 128 : (k + 1) * 128] = onehot(sub == gt[k : k + 1, :])
        ohj_ref[k * 128 : (k + 1) * 128, :] = onehot(wide == g[:, 64 + k : 65 + k])
    adj = dot(ohi_ref[...], ohj_ref[...])
    adj_b = adj.astype(BF16)
    adj_tf = adj.T
    adj_t = adj_tf.astype(BF16)
    mutual = adj * adj_tf
    lane = iota((1, 128), 1)
    rows = iota((32, 128), 0)
    lanes = iota((32, 128), 1)
    number = iota((32, NB), 1)
    in_row = onehot(row_of(number) == iota((32, NB), 0))
    in_col = onehot(col_of(number) == iota((32, NB), 0))
    in_col_t = onehot(col_of(iota((NB, 32), 0)) == iota((NB, 32), 1))

    ci = jnp.full((1, 128), -1.0, F32)
    cj = jnp.full((1, 128), -1.0, F32)
    for s in range(SLOTS):
        shift = (s * 32 + 128 - zl * 32) & 127
        here = (lane >> 5 == s) & ((lane & 31) < N_ROW)
        rows_i = jnp.broadcast_to(gt_ref[pl.ds(u * SLOTS + s, 1), :], (8, 128))
        rows_j = jnp.broadcast_to(gt_ref[pl.ds(64 + u * SLOTS + s, 1), :], (8, 128))
        ci = jnp.where(here, pltpu.roll(rows_i, shift, 1)[0:1], ci)
        cj = jnp.where(here, pltpu.roll(rows_j, shift, 1)[0:1], cj)
    of_i = onehot(sub == ci)
    both = dot(adj_b, onehot(sub == cj)) * dot(adj_b, of_i)
    pairs = jnp.broadcast_to(jnp.sum(mutual, axis=0, keepdims=True), (8, NB)).astype(BF16)
    plain = (ci == cj) & (ci >= 0.0) & (dot(pairs, of_i)[0:1] < 1.5)
    plain_f = jnp.where(plain, 1.0, 0.0)
    wanted = (dot(in_row, both.astype(BF16)) > 0.5) & ((lanes & 31) != rows) & (plain_f < 0.5)
    hit = wanted & ((lanes & 31) == p)
    code = jnp.sum(jnp.where(hit, ((lanes >> 5) + 1).astype(F32), 0.0), axis=1, keepdims=True)
    sends = jnp.where(lanes == 0, code, 0.0)

    li = jnp.full((1, 128), -1.0, F32)
    lk = jnp.full((1, 128), -1.0, F32)
    for z in range(ZL):
        here = (lane >> 5 == z) & ((lane & 31) < SLOTS_ROW)
        mine = jnp.broadcast_to(gij_ref[pl.ds(z * 32 + p, 1), :], (8, 128))
        li = jnp.where(here, (pltpu.roll(mine, z * 32, 1) if z else mine)[0:1], li)
        lk = jnp.where(here, pltpu.roll(mine, (64 + z * 32) % 128, 1)[0:1], lk)
    both = dot(adj_t, onehot(sub == li)) * dot(adj_t, onehot(sub == lk))
    owner = (lanes >> 5) * XC + (((lanes & 31) * 11) >> 5)
    wanted = (dot(in_col, both.astype(BF16)) > 0.5) & (owner != rows) & ((lanes & 31) < SLOTS_ROW)
    wanted = jnp.where(wanted, 1.0, 0.0)
    dl_ref[...] = wanted
    rl_ref[...] = dot(wanted.astype(BF16), onehot((row128 < lane128) & ((row128 >> 5) == (lane128 >> 5))))
    lanes8 = iota((8, 128), 1)
    rows8 = iota((8, 128), 0)
    send_d = jnp.zeros((8, 128), F32)
    send_r = jnp.zeros((8, 128), F32)
    for z in range(ZL):
        send_d = jnp.where(rows8 == z, dl_ref[pl.ds(z * XC + u, 1), :], send_d)
        send_r = jnp.where(rows8 == z, rl_ref[pl.ds(z * XC + u, 1), :], send_r)
    zlist = jnp.zeros((8, 128), F32)
    for c in range(SLOTS):
        hit = (send_d > 0.5) & (send_r == float(c)) & ((lanes8 >> 5) == zl)
        code = jnp.sum(jnp.where(hit, ((lanes8 & 31) + 1).astype(F32), 0.0), axis=1, keepdims=True)
        zlist = jnp.where(lanes8 == c, code, zlist)

    right = jnp.where(ci >= 0.0, (lane + 1).astype(F32), 0.0)
    again = jnp.where(plain, float(PLAIN), right)
    again = jnp.where(((lane & 31) == p) & (ci >= 0.0), (OWN + (lane >> 5)).astype(F32), again)
    stack = jnp.where(row128 == 0, ci, jnp.where(row128 == 1, cj, jnp.where(row128 == 2, right, again))).T
    ci_c, cj_c = stack[:, 0:1], stack[:, 1:2]
    met_c = ci_c == lk
    linked = (jnp.where(met_c, stack[:, 2:3], 0.0), jnp.where(met_c, stack[:, 3:4], 0.0))
    meets = [jnp.zeros((8, 128), F32), jnp.zeros((8, 128), F32)]
    terms = jnp.zeros((8, 128), F32)
    for o in range(SLOTS):
        out_i, out_j = blocks[0, o].astype(F32), blocks[1, o].astype(F32)
        for n in range(2):
            met = jnp.sum(jnp.where(cj_c == out_j, linked[n], 0.0), axis=0, keepdims=True)
            meets[n] = jnp.where(rows8 == o, jnp.where(li == out_i, met, 0.0), meets[n])
        hit = plain & (ci == out_j) & ((lane & 31) != p)
        code = jnp.sum(jnp.where(hit, (lane + 1).astype(F32), 0.0), axis=1, keepdims=True)
        terms = jnp.where((rows8 == o) & (lanes8 == 64), code, terms)
    got_d, got_r = dl_ref[pl.ds(q, 1), :], rl_ref[pl.ds(q, 1), :]
    for t in range(LEFTS):
        if t < ZL * SLOTS:
            hit = (lane >> 5 == t // SLOTS) & (got_d > 0.5) & (got_r == float(t % SLOTS))
        else:
            hit = lane == zl * 32 + u * SLOTS + (t - ZL * SLOTS)
        for n in range(2):
            value = jnp.sum(jnp.where(hit, meets[n], 0.0), axis=1, keepdims=True)
            terms = jnp.where(lanes8 == n * 32 + t, value, terms)

    def per_dev(count):
        return dot(dot(in_row, (count * adj).astype(BF16)).astype(BF16), in_col_t)

    from_i, from_k = iota((NB, NB), 0), iota((NB, NB), 1)
    k_row = row_of(iota((1, NB), 1))
    k_col = col_of(iota((1, NB), 1))
    i_row = row_of(iota((NB, 1), 0))
    i_col = col_of(iota((NB, 1), 0))
    most = jnp.zeros((32, 32), F32)
    to_col = jnp.where(i_col != k_col, adj, 0.0).astype(BF16)
    for z in range(ZL):
        part = jnp.where((k_col >> 3) == z, adj, 0.0).astype(BF16)
        most = jnp.maximum(most, per_dev(dot(part, to_col)))
    left_over = jnp.max(most, keepdims=True) > SLOTS + 0.5
    moving = jnp.where(i_row != k_row, adj, 0.0)
    single = jnp.sum(mutual, axis=1, keepdims=True) < 1.5
    target = jnp.where((from_i == from_k) & single, 0.0, adj).astype(BF16)
    square_row = k_row * k_row
    n, first, high, low = (
        per_dev(dot((moving * weight.astype(F32)).astype(BF16), target))
        for weight in (k_row * 0 + 1, k_row, square_row >> 4, square_row & 15)
    )
    clash = (n > 2.5) | ((n > 1.5) & (2.0 * (16.0 * high + low) == first * first))
    clash = jnp.max(jnp.where(clash, 1.0, 0.0), keepdims=True)
    level = jnp.where(left_over, 2.0, clash)
    zlist = jnp.where((rows8 == 7) & (lanes8 == 0), level, zlist)

    list_ref[0:ZLIST, :] = sends.astype(jnp.int32)
    list_ref[ZLIST:TERMS, :] = zlist.astype(jnp.int32)
    list_ref[TERMS:, :] = terms.astype(jnp.int32)
    copy = pltpu.make_async_copy(list_ref, list_smem, sem)
    copy.start()
    copy.wait()
    for d in range(ZL):
        for c in range(SLOTS):
            code = list_smem[ZLIST + d, c]

            @pl.when(code > 0)
            def _():
                k = code - 1
                src_u = (k * 11) >> 5
                start = pl.multiple_of(src_u * PANEL + (k - src_u * SLOTS) * BLK, 16)
                zbuf_ref[d, c * BLK : (c + 1) * BLK, :] = second_ref[pl.ds(start, BLK), :]


def tile_at(start):
    return pl.ds(pl.multiple_of(start, 16), BLK)


def left_at(t, left_ref, own_ref):
    if t < ZL * SLOTS:
        return left_ref.at[t * BLK : (t + 1) * BLK, :]
    t -= ZL * SLOTS
    return own_ref.at[t * BLK : (t + 1) * BLK, :]


def panel_start(code):
    r = code - 1
    return ((r & 7) * ZH + ((r >> 3) & 3)) * PANEL + (r >> 5) * BLK


def square_kernel(lists, own_ref, left_ref, right_ref, out_ref, diag_ref, send_ref, acc_ref):
    for o in range(SLOTS):
        part = slice(o * BLK, (o + 1) * BLK)
        acc_ref[...] = jnp.zeros((BLK, BLK), F32)
        for t in range(LEFTS):
            code = lists[TERMS + o, t]
            left = left_at(t, left_ref, own_ref)

            @pl.when(code > 0)
            def _():
                acc_ref[...] += dot(left[...], right_ref[tile_at(panel_start(code)), :])

        out_ref[part, :] = acc_ref[...].astype(BF16)
        code = lists[TERMS + o, 64]

        @pl.when(code > 0)
        def _():
            tile = right_ref[tile_at(panel_start(code)), :]
            diag_ref[part, :] = dot(tile, tile).astype(BF16)

    for d in range(N_ROW):
        code = lists[d, 0]

        @pl.when((code > 0) & (code <= SLOTS))
        def _():
            send_ref[d * BLK : (d + 1) * BLK, :] = out_ref[tile_at((code - 1) * BLK), :]


def cube_kernel(room, lists, blocks, own_ref, left_ref, square_ref, diag_ref, right_ref, out_ref, acc_ref):
    for o in range(SLOTS):
        part = slice(o * BLK, (o + 1) * BLK)
        acc_ref[...] = jnp.zeros((BLK, BLK), F32)
        for t in range(LEFTS):
            code = lists[TERMS + o, 32 + t]
            left = left_at(t, left_ref, own_ref)

            @pl.when((code > 0) & (code < OWN))
            def _():
                r = code - 1
                start = (r & 31) * BLK if room == 1 else ((r & 31) * SLOTS + (r >> 5)) * BLK
                acc_ref[...] += dot(left[...], right_ref[tile_at(start), :])

            @pl.when((code >= OWN) & (code < PLAIN))
            def _():
                acc_ref[...] += dot(left[...], square_ref[tile_at((code - OWN) * BLK), :])

            @pl.when(code == PLAIN)
            def _():
                acc_ref[...] += dot(left[...], diag_ref[part, :])

        value = 1.5 * own_ref[part, :].astype(F32) - 0.5 * acc_ref[...]
        out_ref[:, part] = jnp.where(blocks[0, o] >= 0, value, 0.0).astype(BF16)


def swap(value, axes):
    return lax.all_to_all(value, axes, 0, 0, tiled=True)


def like(*shape, dtype=BF16):
    return jax.ShapeDtypeStruct(shape, dtype)


def per_device(x, blocks):
    first, own = pl.pallas_call(
        pack_kernel,
        out_shape=(like(ZH, PANEL, BLK), like(TILES, BLK)),
        in_specs=[SMEM, VMEM], out_specs=(VMEM, VMEM), compiler_params=PARAMS, name="pack",
    )(blocks, x)
    first = swap(first, "zh")
    right = lax.all_gather(first.reshape(ZH * PANEL, BLK), "y", axis=0, tiled=True)
    heads = jnp.sum(first[:, TILES:].astype(F32), axis=0).astype(BF16)
    second = lax.all_gather(jnp.concatenate([own, heads], axis=0), ("x", "c"), axis=0)
    heads = jnp.sum(second[:, TILES:].astype(F32), axis=0).astype(BF16)
    heads = jnp.broadcast_to(heads[None], (Y * ZL, HEAD, 128)).reshape(Y * ZL * HEAD, 128)
    heads = swap(heads, ("y", "zl")).reshape(Y, ZL * HEAD, 128)
    zbuf, lists = pl.pallas_call(
        plan_kernel,
        out_shape=(like(ZL, TILES, BLK), like(TERMS + 8, 128, dtype=jnp.int32)),
        in_specs=[SMEM, VMEM, VMEM], out_specs=(VMEM, VMEM),
        scratch_shapes=[
            pltpu.VMEM((128, 128), F32), pltpu.VMEM((128, 128), F32),
            pltpu.VMEM((NB, SLOTS_ROW * 128), BF16), pltpu.VMEM((SLOTS_ROW * 128, NB), BF16),
            pltpu.VMEM((32, 128), F32), pltpu.VMEM((32, 128), F32),
            pltpu.SMEM((TERMS + 8, 128), jnp.int32), pltpu.SemaphoreType.DMA,
        ],
        compiler_params=PARAMS, name="plan",
    )(blocks, heads, second.reshape(XC * PANEL, BLK))
    left = swap(zbuf, "zl").reshape(ZL * TILES, BLK)
    square, diag, send = pl.pallas_call(
        square_kernel,
        out_shape=(like(TILES, BLK), like(TILES, BLK), like(N_ROW * BLK, BLK)),
        in_specs=[SMEM] + [VMEM] * 3, out_specs=(VMEM,) * 3,
        scratch_shapes=[pltpu.VMEM((BLK, BLK), F32)], compiler_params=PARAMS, name="square",
    )(lists, own, left, right)

    def finish(room, squares):
        return pl.pallas_call(
            lambda *refs: cube_kernel(room, *refs),
            out_shape=like(*x.shape),
            in_specs=[SMEM, SMEM] + [VMEM] * 5, out_specs=VMEM,
            scratch_shapes=[pltpu.VMEM((BLK, BLK), F32)], compiler_params=PARAMS, name="cube%d" % room,
        )(lists, blocks, own, left, square, diag, squares)

    def roomy():
        return finish(SLOTS, swap(jnp.tile(square, (N_ROW, 1)), ROW))

    result = finish(1, swap(send, ROW))
    return lax.switch(lists[TERMS - 1, 0], [lambda: result, roomy, lambda: general(x, blocks)])


def solution(mesh):
    fine = Mesh(mesh.devices.reshape(ZH, Y, ZL, X, C), ROW + COL)
    return jax.shard_map(
        per_device,
        mesh=fine,
        in_specs=(P(ROW, COL), P(ROW, COL)),
        out_specs=P(ROW, COL),
        check_vma=False,
    )
```

time: 379 us -> 149 us (0.39)
  waiting for transfers between devices: 162 us -> 29.6 us
  local copies, waits for them, and re-layouts: 57.9 us -> 2.92 us
  blocking collectives: 124 us -> 81.6 us
  matrix products: 19 us -> 0 us
  Pallas kernels: 0 us -> 14 us
  starting transfers between devices: 0.08 us -> 4.97 us
    all_gather x3 -> x1, waiting for transfers between devices: 161 us -> 0.01 us  [per_device(): lax.all_gather(first.reshape(ZH * PANEL, BLK), 'y', axis=0, tiled=True)]
    all_gather x2 -> x1, blocking collectives: 124 us -> 13.6 us  [per_device(): lax.all_gather(jnp.concatenate([own, heads], axis=0), ('x', 'c'), axis=0)]
    all_to_all x0 -> x3, blocking collectives: none -> 68 us  [swap(): return lax.all_to_all(value, axes, 0, 0, tiled=True)]
    gather x2 -> x0, local copies, waits for them, and re-layouts: 38 us -> none  [left_fold(): right_grid[partner_slot // slot_count, :, partner_slot % slot_count, :]]
    all_to_all x0 -> x1, waiting for transfers between devices: none -> 29.6 us  [swap(): return lax.all_to_all(value, axes, 0, 0, tiled=True)]
    dot_general x2 -> x0, matrix products: 19 us -> none  [left_fold(): jnp.einsum('iak,aokj->ioj', left_list, picked, preferred_element_type=jnp...]
    pallas_call x0 -> x4, Pallas kernels: none -> 14 us  [the longest x1 8.3 us: per_device(): pl.pallas_call(plan_kernel, out_shape=(like(ZL, TILES, BLK), like(TERMS +...]
    reshape x3 -> x0, local copies, waits for them, and re-layouts: 12.8 us -> none  [left_fold(): right_grid = panel.reshape(panel_rows, block_size, slot_count, block_size)]
  transfers between devices with their start and end apart: 3 -> 2, of which waited for: 3 -> 1; matrix products, arithmetic and copies ran while one was open for 9% -> 1% of each run, Pallas kernels for 0% -> 6%
where the time goes in v2:
time: 149 us; the launch traced here: 148 us
  blocking collectives  81.6 us (55%)
  waiting for transfers between devices  29.6 us (20%)
  between operations  14.1 us (9%)
  Pallas kernels  14 us (9%)
  starting transfers between devices  4.97 us (3%)
  local copies, waits for them, and re-layouts  2.92 us (2%)
    all_to_all x3, blocking collectives, swap(): return lax.all_to_all(value, axes, 0, 0, tiled=True)  68 us
    all_to_all x1, waiting for transfers between devices, swap(): return lax.all_to_all(value, axes, 0, 0, tiled=True)  29.6 us
    all_gather x1, blocking collectives, per_device(): lax.all_gather(jnp.concatenate([own, heads], axis=0), ('x', 'c'), axis=0)  13.6 us
    pallas_call x1, Pallas kernels, per_device(): pl.pallas_call(plan_kernel, out_shape=(like(ZL, TILES, BLK), like(TERMS +...  8.3 us
    all_to_all x1, starting transfers between devices, swap(): return lax.all_to_all(value, axes, 0, 0, tiled=True)  4.97 us
  transfers between devices with their start and end apart: 2, of which 1 were waited for; matrix products, arithmetic and copies ran while one was open for 1% of the time, Pallas kernels for 6%

profile of v2, /device:TPU:6, one launch (start us, length us, event | category | flops | bytes accessed | tf_op | source)
XLA Modules:
  0.0 148.2 jit_solution(839651510334892071)
XLA Ops:
  6.5 0.0 copy-start.4
  6.5 0.0 copy-start.2
  6.5 0.0 all-gather.14.cloned.1.call-start
  6.5 1.0 pack.1
  7.6 28.2 %all_to_all.34 = bf16[3,416,128]{2,1,0:T(8,128)(2,1)} all-to-all(bf16[3,416,128]{2,1,0:T(8,128)(2,1)S(1)} %get-tuple-element.42), channel_id=1, replica_groups=mesh['zh'=3,'y'=8,'zl'=4,'x'=4,'c'=2] {'zh'}, dimensions={0} | all-to-all | bytes 638976 | tf_op jit(solution)/shard_map/all_to_all | solution.py:350
  35.8 0.0 all-gather.14.cloned.1.call-update
  35.8 0.7 slice_reduce_fusion.3
  36.6 13.6 %all-gather.second_ref = bf16[3328,128]{1,0:T(8,128)(2,1)S(1)} all-gather(bf16[416,128]{1,0:T(8,128)(2,1)S(1)} %pad_maximum_fusion), channel_id=2, replica_groups=mesh['zh'=3,'y'=8,'zl'=4,'x'=4,'c'=2] {'x','c'}, dimensions={0}, use_global_device_ids=true | all-gather | bytes 958464 | tf_op jit(solution)/shard_map/all_gather | solution.py:366
  50.2 24.3 %all_to_all.35 = bf16[32,32,128]{2,1,0:T(8,128)(2,1)S(1)} all-to-all(bf16[32,32,128]{2,1,0:T(8,128)(2,1)S(1)} %broadcast_in_dim.43), channel_id=1, replica_groups=mesh['zh'=3,'y'=8,'zl'=4,'x'=4,'c'=2] {'y','zl'}, dimensions={0} | all-to-all | bytes 524288 | tf_op jit(solution)/shard_map/all_to_all | solution.py:350
  74.5 8.3 %plan.1 = (bf16[4,384,128]{2,1,0:T(8,128)(2,1)S(1)}, s32[48,128]{1,0:T(8,128)S(1)}) custom-call(s32[2,3]{1,0:T(2,128)} %refs_1_.1, bf16[8,128,128]{2,1,0:T(8,128)(2,1)S(1)} %bitcast.91, bf16[3328,128]{1,0:T(8,128)(2,1)S(1)} %all-gather.second_ref), custom_call_target="tpu_custom_call" | custom-call | tf_op jit(solution)/shard_map/plan/pallas_call | solution.py:370
  82.8 15.5 %all_to_all.36 = bf16[4,384,128]{2,1,0:T(8,128)(2,1)S(1)} all-to-all(bf16[4,384,128]{2,1,0:T(8,128)(2,1)S(1)} %get-tuple-element.44), channel_id=1, replica_groups=mesh['zh'=3,'y'=8,'zl'=4,'x'=4,'c'=2] {'zl'}, dimensions={0} | all-to-all | bytes 786432 | tf_op jit(solution)/shard_map/all_to_all | solution.py:350
  98.3 0.0 all-gather.14.cloned.1.call-done.right_ref
  98.3 0.0 copy-start
  98.3 1.7 %copy-done = bf16[9984,128]{1,0:T(8,128)(2,1)S(1)} copy-done((bf16[9984,128]{1,0:T(8,128)(2,1)S(1)}, bf16[9984,128]{1,0:T(8,128)(2,1)}, u32[]{:S(2)}) %copy-start) | copy-done | bytes 2555928
  100.0 2.6 %square.1 = (bf16[384,128]{1,0:T(8,128)(2,1)S(1)}, bf16[384,128]{1,0:T(8,128)(2,1)S(1)}, bf16[3072,128]{1,0:T(8,128)(2,1)}) custom-call(s32[48,128]{1,0:T(8,128)S(1)} %get-tuple-element.43.lists.refs_0_, bf16[384,128]{1,0:T(8,128)(2,1)S(1)} %get-tuple-element.41.own_ref.refs_2_, bf16[1536,128]{1,0:T(8,128)(2,1)S(1)} %bitcast.96, bf16[9984,128]{1,0:T(8,128)(2,1)S(1)} %copy-done), custom_call_target="tpu_custom_call" | custom-call | tf_op jit(solution)/shard_map/square/pallas_call | solution.py:383
  102.7 5.0 %all-to-all-start.4 = ((bf16[24,128,128]{2,1,0:T(8,128)(2,1)}), bf16[24,128,128]{2,1,0:T(8,128)(2,1)S(1)}, u32[]{:S(2)}, u32[]{:S(2)}) async-start(bf16[24,128,128]{2,1,0:T(8,128)(2,1)} %bitcast.29), calls=%async_computation.4 | async-start | bytes 1572864 | tf_op jit(solution)/shard_map/all_to_all | solution.py:350
  107.6 0.5 slice.36
  108.8 29.6 %all-to-all-done.4 = bf16[24,128,128]{2,1,0:T(8,128)(2,1)S(1)} async-done(((bf16[24,128,128]{2,1,0:T(8,128)(2,1)}), bf16[24,128,128]{2,1,0:T(8,128)(2,1)S(1)}, u32[]{:S(2)}, u32[]{:S(2)}) %all-to-all-start.4) | async-done | bytes 786464 | tf_op jit(solution)/shard_map/all_to_all | solution.py:350
  138.4 0.0 copy-done.4
  138.4 2.0 %cube1.1 = bf16[128,384]{1,0:T(8,128)(2,1)S(1)} custom-call(s32[48,128]{1,0:T(8,128)S(1)} %get-tuple-element.43.lists.refs_0_, s32[2,3]{1,0:T(2,128)S(1)} %copy-done.4, bf16[384,128]{1,0:T(8,128)(2,1)S(1)} %get-tuple-element.41.own_ref.refs_2_, bf16[1536,128]{1,0:T(8,128)(2,1)S(1)} %bitcast.97, bf16[384,128]{1,0:T(8,128)(2,1)S(1)} %get-tuple-element.45.refs_4_, ...), custom_call_target="tpu_custom_call" | custom-call | tf_op jit(solution)/shard_map/cube1/pallas_call | solution.py:391
  140.4 0.0 copy-done.2
  140.4 0.3 conditional.1
  140.8 0.0 copy-start.3
  140.8 0.6 copy-done.3
  (3 shorter events, 0.1 us)
Async XLA Ops:
  6.5 131.9 %copy-start.4 = (s32[2,3]{1,0:T(2,128)S(1)}, s32[2,3]{1,0:T(2,128)}, u32[]{:S(2)}) copy-start(s32[2,3]{1,0:T(2,128)} %refs_1_.1) | copy-start | bytes 76
  6.5 133.9 %copy-start.2 = (bf16[128,384]{1,0:T(8,128)(2,1)S(1)}, bf16[128,384]{1,0:T(8,128)(2,1)}, u32[]{:S(2)}) copy-start(bf16[128,384]{1,0:T(8,128)(2,1)} %x_ref.1) | copy-start | bytes 294916
  6.5 91.8 %all-gather.14.cloned.1.call-start = ((), (), s32[]{:S(2)}) async-start(), calls=%async_computation.8 | async-start | bytes 2875392 | tf_op jit(solution)/shard_map/all_gather | solution.py:364
  98.3 1.7 %copy-start = (bf16[9984,128]{1,0:T(8,128)(2,1)S(1)}, bf16[9984,128]{1,0:T(8,128)(2,1)}, u32[]{:S(2)}) copy-start(bf16[9984,128]{1,0:T(8,128)(2,1)} %all-gather.14.cloned.1.call-done.right_ref) | copy-start | bytes 7667716
  102.7 35.7 %all-to-all-start.4 = ((bf16[24,128,128]{2,1,0:T(8,128)(2,1)}), bf16[24,128,128]{2,1,0:T(8,128)(2,1)S(1)}, u32[]{:S(2)}, u32[]{:S(2)}) async-start(bf16[24,128,128]{2,1,0:T(8,128)(2,1)} %bitcast.29), calls=%async_computation.4 | async-start | bytes 1572864 | tf_op jit(solution)/shard_map/all_to_all | solution.py:350
  140.8 0.6 copy-start.3
Sparse Core Ops, SparseCore 0:
  35.9 50.1 all-gather.13

commit v3 on v2

--- a/solution.py
+++ b/solution.py
@@ -12,7 +12,7 @@
 N_ROW, N_COL = ZH * Y, ZL * XC
 SLOTS = 3
 TILES = SLOTS * BLK
-HEAD = 32
+HEAD = 16
 PANEL = TILES + HEAD
 SLOTS_ROW = XC * SLOTS
 LEFTS = ZL * SLOTS + SLOTS
@@ -112,7 +112,7 @@
 def pack_kernel(blocks, x_ref, out_ref, own_ref):
     zh, y, zl, u, p, q = place()
     lane = iota((HEAD, 128), 1)
-    here = iota((HEAD, 128), 0) == p
+    here = iota((HEAD, 128), 0) == zh
     head = jnp.zeros((HEAD, 128), F32)
     for s in range(SLOTS):
         for v in range(4):
@@ -134,7 +134,12 @@
     gij_ref, gt_ref, ohi_ref, ohj_ref, dl_ref, rl_ref, list_smem, sem,
 ):
     zh, y, zl, u, p, q = place()
-    g = jnp.sum(g_ref[...].astype(F32), axis=0)
+    told = g_ref[...].astype(F32)
+    for z in range(ZL):
+        for h in range(ZH):
+            gij_ref[z * 32 + h * Y : z * 32 + (h + 1) * Y, :] = told[:, z * HEAD + h, :]
+        gij_ref[z * 32 + N_ROW : (z + 1) * 32, :] = jnp.zeros((32 - N_ROW, 128), F32)
+    g = gij_ref[...]
     g = 16.0 * g + pltpu.roll(g, 96, 1)
     row128, lane128 = iota((128, 128), 0), iota((128, 128), 1)
     g = jnp.where(((row128 & 31) < N_ROW) & ((lane128 & 63) < SLOTS_ROW), g, -1.0)
@@ -248,12 +253,12 @@
     moving = jnp.where(i_row != k_row, adj, 0.0)
     single = jnp.sum(mutual, axis=1, keepdims=True) < 1.5
     target = jnp.where((from_i == from_k) & single, 0.0, adj).astype(BF16)
-    square_row = k_row * k_row
-    n, first, high, low = (
+    n, first, second = (
         per_dev(dot((moving * weight.astype(F32)).astype(BF16), target))
-        for weight in (k_row * 0 + 1, k_row, square_row >> 4, square_row & 15)
+        for weight in (k_row * 0 + 1, k_row, ((k_row - 11) * (k_row - 12)) >> 1)
     )
-    clash = (n > 2.5) | ((n > 1.5) & (2.0 * (16.0 * high + low) == first * first))
+    half = 0.5 * first
+    clash = (n > 2.5) | ((n > 1.5) & ((half - 11.0) * (half - 12.0) == second))
     clash = jnp.max(jnp.where(clash, 1.0, 0.0), keepdims=True)
     level = jnp.where(left_over, 2.0, clash)
     zlist = jnp.where((rows8 == 7) & (lanes8 == 0), level, zlist)
@@ -292,7 +297,7 @@
     return ((r & 7) * ZH + ((r >> 3) & 3)) * PANEL + (r >> 5) * BLK
 
 
-def square_kernel(lists, own_ref, left_ref, right_ref, out_ref, diag_ref, send_ref, acc_ref):
+def square_kernel(lists, own_ref, left_ref, right_ref, out_ref, acc_ref):
     for o in range(SLOTS):
         part = slice(o * BLK, (o + 1) * BLK)
         acc_ref[...] = jnp.zeros((BLK, BLK), F32)
@@ -310,17 +315,19 @@
         @pl.when(code > 0)
         def _():
             tile = right_ref[tile_at(panel_start(code)), :]
-            diag_ref[part, :] = dot(tile, tile).astype(BF16)
-
+            out_ref[TILES + o * BLK : TILES + (o + 1) * BLK, :] = dot(tile, tile).astype(BF16)
+
+
+def send_kernel(lists, square_ref, send_ref):
     for d in range(N_ROW):
         code = lists[d, 0]
 
         @pl.when((code > 0) & (code <= SLOTS))
         def _():
-            send_ref[d * BLK : (d + 1) * BLK, :] = out_ref[tile_at((code - 1) * BLK), :]
-
-
-def cube_kernel(room, lists, blocks, own_ref, left_ref, square_ref, diag_ref, right_ref, out_ref, acc_ref):
+            send_ref[d] = square_ref[tile_at((code - 1) * BLK), :]
+
+
+def cube_kernel(room, lists, blocks, own_ref, left_ref, square_ref, right_ref, out_ref, level_ref, acc_ref):
     for o in range(SLOTS):
         part = slice(o * BLK, (o + 1) * BLK)
         acc_ref[...] = jnp.zeros((BLK, BLK), F32)
@@ -340,10 +347,11 @@
 
             @pl.when(code == PLAIN)
             def _():
-                acc_ref[...] += dot(left[...], diag_ref[part, :])
+                acc_ref[...] += dot(left[...], square_ref[TILES + o * BLK : TILES + (o + 1) * BLK, :])
 
         value = 1.5 * own_ref[part, :].astype(F32) - 0.5 * acc_ref[...]
         out_ref[:, part] = jnp.where(blocks[0, o] >= 0, value, 0.0).astype(BF16)
+    level_ref[0] = lists[TERMS - 1, 0]
 
 
 def swap(value, axes):
@@ -380,26 +388,35 @@
         compiler_params=PARAMS, name="plan",
     )(blocks, heads, second.reshape(XC * PANEL, BLK))
     left = swap(zbuf, "zl").reshape(ZL * TILES, BLK)
-    square, diag, send = pl.pallas_call(
+    square = pl.pallas_call(
         square_kernel,
-        out_shape=(like(TILES, BLK), like(TILES, BLK), like(N_ROW * BLK, BLK)),
-        in_specs=[SMEM] + [VMEM] * 3, out_specs=(VMEM,) * 3,
+        out_shape=like(2 * TILES, BLK),
+        in_specs=[SMEM] + [VMEM] * 3, out_specs=VMEM,
         scratch_shapes=[pltpu.VMEM((BLK, BLK), F32)], compiler_params=PARAMS, name="square",
     )(lists, own, left, right)
-
-    def finish(room, squares):
+    send = pl.pallas_call(
+        send_kernel,
+        out_shape=like(N_ROW, BLK, BLK),
+        in_specs=[SMEM, VMEM], out_specs=VMEM, compiler_params=PARAMS, name="send",
+    )(lists, square)
+
+    def finish(room, squares, lists, blocks, own, left, square):
         return pl.pallas_call(
             lambda *refs: cube_kernel(room, *refs),
-            out_shape=like(*x.shape),
-            in_specs=[SMEM, SMEM] + [VMEM] * 5, out_specs=VMEM,
+            out_shape=(like(*x.shape), like(1, dtype=jnp.int32)),
+            in_specs=[SMEM, SMEM] + [VMEM] * 4, out_specs=(VMEM, SMEM),
             scratch_shapes=[pltpu.VMEM((BLK, BLK), F32)], compiler_params=PARAMS, name="cube%d" % room,
-        )(lists, blocks, own, left, square, diag, squares)
+        )(lists, blocks, own, left, square, squares)
+
+
+    kept = (lists, blocks, own, left, square)
+    result, level = finish(1, swap(send, ROW).reshape(N_ROW * BLK, BLK), *kept)
+    result, level, x, kept = lax.optimization_barrier((result, level, x, kept))
 
     def roomy():
-        return finish(SLOTS, swap(jnp.tile(square, (N_ROW, 1)), ROW))
-
-    result = finish(1, swap(send, ROW))
-    return lax.switch(lists[TERMS - 1, 0], [lambda: result, roomy, lambda: general(x, blocks)])
+        return finish(SLOTS, swap(jnp.tile(kept[-1][:TILES], (N_ROW, 1)), ROW), *kept)[0]
+
+    return lax.switch(level[0], [lambda: result, roomy, lambda: general(x, kept[1])])
 
 
 def solution(mesh):

time: 149 us -> 145 us (0.973)
  blocking collectives: 81.6 us -> 113 us
  waiting for transfers between devices: 29.6 us -> 0.02 us
  starting transfers between devices: 4.97 us -> 0.01 us
    all_to_all x3 -> x4, blocking collectives: 68 us -> 99.4 us  [swap(): return lax.all_to_all(value, axes, 0, 0, tiled=True)]
    all_to_all x1 -> x0, waiting for transfers between devices: 29.6 us -> none  [swap(): return lax.all_to_all(value, axes, 0, 0, tiled=True)]
    all_to_all x1 -> x0, starting transfers between devices: 4.97 us -> none  [swap(): return lax.all_to_all(value, axes, 0, 0, tiled=True)]
    pallas_call x2 -> x3, Pallas kernels: 4.64 us -> 5.26 us  [the longest x1 2.47 us: finish(): pl.pallas_call(lambda *refs: cube_kernel(room, *refs), out_shape=(like(*x...]
  transfers between devices with their start and end apart: 2 -> 1, of which waited for: 1 -> 0; matrix products, arithmetic and copies ran while one was open for 1% -> 1% of each run, Pallas kernels for 6% -> 5%
where the time goes in v3:
time: 145 us
  blocking collectives  113 us (78%)
  Pallas kernels  14.1 us (10%)
  between operations  14.1 us (10%)
  local copies, waits for them, and re-layouts  2.36 us (2%)
    all_to_all x4, blocking collectives, swap(): return lax.all_to_all(value, axes, 0, 0, tiled=True)  99.4 us
    all_gather x1, blocking collectives, per_device(): lax.all_gather(jnp.concatenate([own, heads], axis=0), ('x', 'c'), axis=0)  13.5 us
    pallas_call x1, Pallas kernels, per_device(): pl.pallas_call(plan_kernel, out_shape=(like(ZL, TILES, BLK), like(TERMS +...  7.81 us
  transfers between devices with their start and end apart: 1, of which 0 were waited for; matrix products, arithmetic and copies ran while one was open for 1% of the time, Pallas kernels for 5%

profile of v3, /device:TPU:6, one launch (start us, length us, event | category | flops | bytes accessed | tf_op | source)
XLA Modules:
  0.0 144.6 jit_solution(16865847469070628832)
XLA Ops:
  6.5 0.0 copy-start.3
  6.5 0.0 copy-start.2
  6.5 0.0 all-gather.14.cloned.1.call-start
  6.5 1.0 pack.1
  7.6 28.0 %all_to_all.28 = bf16[3,400,128]{2,1,0:T(8,128)(2,1)} all-to-all(bf16[3,400,128]{2,1,0:T(8,128)(2,1)S(1)} %get-tuple-element.47), channel_id=1, replica_groups=mesh['zh'=3,'y'=8,'zl'=4,'x'=4,'c'=2] {'zh'}, dimensions={0} | all-to-all | bytes 614400 | tf_op jit(solution)/shard_map/all_to_all | solution.py:358
  35.6 0.0 all-gather.14.cloned.1.call-update
  35.6 0.7 slice_reduce_fusion.3
  36.3 13.5 %all-gather.second_ref = bf16[3200,128]{1,0:T(8,128)(2,1)S(1)} all-gather(bf16[400,128]{1,0:T(8,128)(2,1)S(1)} %pad_maximum_fusion), channel_id=2, replica_groups=mesh['zh'=3,'y'=8,'zl'=4,'x'=4,'c'=2] {'x','c'}, dimensions={0}, use_global_device_ids=true | all-gather | bytes 921600 | tf_op jit(solution)/shard_map/all_gather | solution.py:374
  49.9 22.0 %all_to_all.29 = bf16[32,16,128]{2,1,0:T(8,128)(2,1)S(1)} all-to-all(bf16[32,16,128]{2,1,0:T(8,128)(2,1)S(1)} %broadcast_in_dim.43), channel_id=1, replica_groups=mesh['zh'=3,'y'=8,'zl'=4,'x'=4,'c'=2] {'y','zl'}, dimensions={0} | all-to-all | bytes 262144 | tf_op jit(solution)/shard_map/all_to_all | solution.py:358
  71.9 7.8 %plan.1 = (bf16[4,384,128]{2,1,0:T(8,128)(2,1)S(1)}, s32[48,128]{1,0:T(8,128)S(1)}) custom-call(s32[2,3]{1,0:T(2,128)} %refs_1_.1, bf16[8,64,128]{2,1,0:T(8,128)(2,1)S(1)} %bitcast.90, bf16[3200,128]{1,0:T(8,128)(2,1)S(1)} %all-gather.second_ref), custom_call_target="tpu_custom_call" | custom-call | tf_op jit(solution)/shard_map/plan/pallas_call | solution.py:378
  79.8 13.9 %all_to_all.30 = bf16[4,384,128]{2,1,0:T(8,128)(2,1)S(1)} all-to-all(bf16[4,384,128]{2,1,0:T(8,128)(2,1)S(1)} %get-tuple-element.49), channel_id=1, replica_groups=mesh['zh'=3,'y'=8,'zl'=4,'x'=4,'c'=2] {'zl'}, dimensions={0} | all-to-all | bytes 786432 | tf_op jit(solution)/shard_map/all_to_all | solution.py:358
  93.6 0.0 all-gather.14.cloned.1.call-done.right_ref
  93.7 0.0 copy-start
  93.7 1.7 %copy-done = bf16[9600,128]{1,0:T(8,128)(2,1)S(1)} copy-done((bf16[9600,128]{1,0:T(8,128)(2,1)S(1)}, bf16[9600,128]{1,0:T(8,128)(2,1)}, u32[]{:S(2)}) %copy-start) | copy-done | bytes 2457624
  95.3 1.6 %square.1.square_ref.refs_4_ = bf16[768,128]{1,0:T(8,128)(2,1)S(1)} custom-call(s32[48,128]{1,0:T(8,128)S(1)} %get-tuple-element.55.lists.refs_0_, bf16[384,128]{1,0:T(8,128)(2,1)S(1)} %get-tuple-element.57.own_ref.refs_2_, bf16[1536,128]{1,0:T(8,128)(2,1)S(1)} %bitcast.95, bf16[9600,128]{1,0:T(8,128)(2,1)S(1)} %copy-done), custom_call_target="tpu_custom_call" | custom-call | tf_op jit(solution)/shard_map/square/pallas_call | solution.py:391
  97.0 1.2 send.1
  98.2 35.5 %all_to_all.31 = bf16[24,128,128]{2,1,0:T(8,128)(2,1)S(1)} all-to-all(bf16[24,128,128]{2,1,0:T(8,128)(2,1)S(1)} %send.1), channel_id=1, replica_groups=mesh['zh'=3,'y'=8,'zl'=4,'x'=4,'c'=2] {'zh','y'}, dimensions={0} | all-to-all | bytes 1572864 | tf_op jit(solution)/shard_map/all_to_all | solution.py:358
  133.6 0.0 copy-done.3
  133.6 2.5 %cube1.1 = (bf16[128,384]{1,0:T(8,128)(2,1)S(1)}, s32[1]{0:T(128)}) custom-call(s32[48,128]{1,0:T(8,128)S(1)} %get-tuple-element.55.lists.refs_0_, s32[2,3]{1,0:T(2,128)S(1)} %copy-done.3, bf16[384,128]{1,0:T(8,128)(2,1)S(1)} %get-tuple-element.57.own_ref.refs_2_, bf16[1536,128]{1,0:T(8,128)(2,1)S(1)} %bitcast.96, ...), custom_call_target="tpu_custom_call" | custom-call | tf_op jit(solution)/shard_map/cube1/pallas_call | solution.py:404
  136.8 0.0 copy-done.2
  136.8 0.3 conditional.1
  137.1 0.0 copy-start.4
  137.1 0.6 copy-done.4
  (3 shorter events, 0.0 us)
Async XLA Ops:
  6.5 127.1 %copy-start.3 = (s32[2,3]{1,0:T(2,128)S(1)}, s32[2,3]{1,0:T(2,128)}, u32[]{:S(2)}) copy-start(s32[2,3]{1,0:T(2,128)} %refs_1_.1) | copy-start | bytes 76
  6.5 130.2 %copy-start.2 = (bf16[128,384]{1,0:T(8,128)(2,1)S(1)}, bf16[128,384]{1,0:T(8,128)(2,1)}, u32[]{:S(2)}) copy-start(bf16[128,384]{1,0:T(8,128)(2,1)} %x_ref.1) | copy-start | bytes 294916
  6.5 87.1 %all-gather.14.cloned.1.call-start = ((), (), s32[]{:S(2)}) async-start(), calls=%async_computation.8 | async-start | bytes 2764800 | tf_op jit(solution)/shard_map/all_gather | solution.py:372
  93.7 1.7 %copy-start = (bf16[9600,128]{1,0:T(8,128)(2,1)S(1)}, bf16[9600,128]{1,0:T(8,128)(2,1)}, u32[]{:S(2)}) copy-start(bf16[9600,128]{1,0:T(8,128)(2,1)} %all-gather.14.cloned.1.call-done.right_ref) | copy-start | bytes 7372804
  137.1 0.6 copy-start.4
Sparse Core Ops, SparseCore 0:
  35.7 46.5 all-gather.13

commit v4 on v3

--- a/solution.py
+++ b/solution.py
@@ -17,7 +17,8 @@
 SLOTS_ROW = XC * SLOTS
 LEFTS = ZL * SLOTS + SLOTS
 OWN, PLAIN = 128, 160
-ZLIST, TERMS = 32, 40
+ROOM = 2
+ZLIST, TERMS = 8, 16
 ROW = ("zh", "y")
 COL = ("zl", "x", "c")
 F32 = jnp.float32
@@ -131,7 +132,7 @@
 
 def plan_kernel(
     blocks, g_ref, second_ref, zbuf_ref, list_ref,
-    gij_ref, gt_ref, ohi_ref, ohj_ref, dl_ref, rl_ref, list_smem, sem,
+    gij_ref, gt_ref, ohi_ref, ohj_ref, dy_ref, ry_ref, dl_ref, rl_ref, list_smem, sem,
 ):
     zh, y, zl, u, p, q = place()
     told = g_ref[...].astype(F32)
@@ -179,9 +180,18 @@
     plain = (ci == cj) & (ci >= 0.0) & (dot(pairs, of_i)[0:1] < 1.5)
     plain_f = jnp.where(plain, 1.0, 0.0)
     wanted = (dot(in_row, both.astype(BF16)) > 0.5) & ((lanes & 31) != rows) & (plain_f < 0.5)
-    hit = wanted & ((lanes & 31) == p)
-    code = jnp.sum(jnp.where(hit, ((lanes >> 5) + 1).astype(F32), 0.0), axis=1, keepdims=True)
-    sends = jnp.where(lanes == 0, code, 0.0)
+    wanted = jnp.where(wanted, 1.0, 0.0)
+    dy_ref[...] = wanted
+    ry_ref[...] = dot(wanted.astype(BF16), onehot((row128 < lane128) & ((row128 & 7) == (lane128 & 7))))
+    lanes8 = iota((8, 128), 1)
+    rows8 = iota((8, 128), 0)
+    send_d = dy_ref[pl.ds(pl.multiple_of(zh * Y, 8), 8), :]
+    send_r = ry_ref[pl.ds(pl.multiple_of(zh * Y, 8), 8), :]
+    ylist = jnp.zeros((8, 128), F32)
+    for c in range(ROOM):
+        hit = (send_d > 0.5) & (send_r == float(c)) & ((lanes8 & 7) == y)
+        code = jnp.sum(jnp.where(hit, (lanes8 + 1).astype(F32), 0.0), axis=1, keepdims=True)
+        ylist = jnp.where(lanes8 == c, code, ylist)
 
     li = jnp.full((1, 128), -1.0, F32)
     lk = jnp.full((1, 128), -1.0, F32)
@@ -196,8 +206,6 @@
     wanted = jnp.where(wanted, 1.0, 0.0)
     dl_ref[...] = wanted
     rl_ref[...] = dot(wanted.astype(BF16), onehot((row128 < lane128) & ((row128 >> 5) == (lane128 >> 5))))
-    lanes8 = iota((8, 128), 1)
-    rows8 = iota((8, 128), 0)
     send_d = jnp.zeros((8, 128), F32)
     send_r = jnp.zeros((8, 128), F32)
     for z in range(ZL):
@@ -210,7 +218,9 @@
         zlist = jnp.where(lanes8 == c, code, zlist)
 
     right = jnp.where(ci >= 0.0, (lane + 1).astype(F32), 0.0)
-    again = jnp.where(plain, float(PLAIN), right)
+    got_d, got_r = dy_ref[pl.ds(p, 1), :], ry_ref[pl.ds(p, 1), :]
+    again = jnp.where(got_d > 0.5, ((lane & 7) * ROOM + 1).astype(F32) + got_r, 0.0)
+    again = jnp.where(plain, float(PLAIN), again)
     again = jnp.where(((lane & 31) == p) & (ci >= 0.0), (OWN + (lane >> 5)).astype(F32), again)
     stack = jnp.where(row128 == 0, ci, jnp.where(row128 == 1, cj, jnp.where(row128 == 2, right, again))).T
     ci_c, cj_c = stack[:, 0:1], stack[:, 1:2]
@@ -244,26 +254,29 @@
     k_col = col_of(iota((1, NB), 1))
     i_row = row_of(iota((NB, 1), 0))
     i_col = col_of(iota((NB, 1), 0))
-    most = jnp.zeros((32, 32), F32)
+    def fullest(total, parts, room):
+        least = total
+        for part in parts:
+            least = jnp.minimum(least, jnp.maximum(part, total - part))
+        return jnp.max(jnp.where(least > room + 0.5, 1.0, 0.0), keepdims=True)
+
     to_col = jnp.where(i_col != k_col, adj, 0.0).astype(BF16)
-    for z in range(ZL):
-        part = jnp.where((k_col >> 3) == z, adj, 0.0).astype(BF16)
-        most = jnp.maximum(most, per_dev(dot(part, to_col)))
-    left_over = jnp.max(most, keepdims=True) > SLOTS + 0.5
+    total = per_dev(dot(adj_b, to_col))
+    parts = [
+        per_dev(dot(jnp.where(((k_col >> bit) & 1) == 1, adj, 0.0).astype(BF16), to_col)) for bit in (3, 4)
+    ]
+    over = fullest(total, parts, SLOTS)
     moving = jnp.where(i_row != k_row, adj, 0.0)
     single = jnp.sum(mutual, axis=1, keepdims=True) < 1.5
     target = jnp.where((from_i == from_k) & single, 0.0, adj).astype(BF16)
-    n, first, second = (
-        per_dev(dot((moving * weight.astype(F32)).astype(BF16), target))
-        for weight in (k_row * 0 + 1, k_row, ((k_row - 11) * (k_row - 12)) >> 1)
-    )
-    half = 0.5 * first
-    clash = (n > 2.5) | ((n > 1.5) & ((half - 11.0) * (half - 12.0) == second))
-    clash = jnp.max(jnp.where(clash, 1.0, 0.0), keepdims=True)
-    level = jnp.where(left_over, 2.0, clash)
-    zlist = jnp.where((rows8 == 7) & (lanes8 == 0), level, zlist)
-
-    list_ref[0:ZLIST, :] = sends.astype(jnp.int32)
+    total = per_dev(dot(moving.astype(BF16), target))
+    parts = [
+        per_dev(dot(jnp.where(((k_row >> bit) & 1) == 1, moving, 0.0).astype(BF16), target)) for bit in (0, 1, 2)
+    ]
+    over = jnp.maximum(over, fullest(total, parts, ROOM))
+    zlist = jnp.where((rows8 == 7) & (lanes8 == 0), over, zlist)
+
+    list_ref[0:ZLIST, :] = ylist.astype(jnp.int32)
     list_ref[ZLIST:TERMS, :] = zlist.astype(jnp.int32)
     list_ref[TERMS:, :] = terms.astype(jnp.int32)
     copy = pltpu.make_async_copy(list_ref, list_smem, sem)
@@ -297,7 +310,7 @@
     return ((r & 7) * ZH + ((r >> 3) & 3)) * PANEL + (r >> 5) * BLK
 
 
-def square_kernel(lists, own_ref, left_ref, right_ref, out_ref, acc_ref):
+def square_kernel(lists, own_ref, left_ref, right_ref, out_ref, near_ref, acc_ref):
     for o in range(SLOTS):
         part = slice(o * BLK, (o + 1) * BLK)
         acc_ref[...] = jnp.zeros((BLK, BLK), F32)
@@ -309,25 +322,31 @@
             def _():
                 acc_ref[...] += dot(left[...], right_ref[tile_at(panel_start(code)), :])
 
-        out_ref[part, :] = acc_ref[...].astype(BF16)
+        tile = acc_ref[...].astype(BF16)
+        near_ref[part, :] = tile
+        for z in range(ZH):
+            out_ref[z, part, :] = tile
         code = lists[TERMS + o, 64]
 
         @pl.when(code > 0)
         def _():
             tile = right_ref[tile_at(panel_start(code)), :]
-            out_ref[TILES + o * BLK : TILES + (o + 1) * BLK, :] = dot(tile, tile).astype(BF16)
+            near_ref[TILES + o * BLK : TILES + (o + 1) * BLK, :] = dot(tile, tile).astype(BF16)
 
 
 def send_kernel(lists, square_ref, send_ref):
-    for d in range(N_ROW):
-        code = lists[d, 0]
-
-        @pl.when((code > 0) & (code <= SLOTS))
-        def _():
-            send_ref[d] = square_ref[tile_at((code - 1) * BLK), :]
-
-
-def cube_kernel(room, lists, blocks, own_ref, left_ref, square_ref, right_ref, out_ref, level_ref, acc_ref):
+    for d in range(Y):
+        for c in range(ROOM):
+            code = lists[d, c]
+
+            @pl.when(code > 0)
+            def _():
+                r = code - 1
+                start = ((r >> 3) & 3) * TILES + (r >> 5) * BLK
+                send_ref[d, c * BLK : (c + 1) * BLK, :] = square_ref[tile_at(start), :]
+
+
+def cube_kernel(lists, blocks, own_ref, left_ref, near_ref, right_ref, out_ref, level_ref, acc_ref):
     for o in range(SLOTS):
         part = slice(o * BLK, (o + 1) * BLK)
         acc_ref[...] = jnp.zeros((BLK, BLK), F32)
@@ -335,19 +354,14 @@
             code = lists[TERMS + o, 32 + t]
             left = left_at(t, left_ref, own_ref)
 
-            @pl.when((code > 0) & (code < OWN))
+            @pl.when((code > 0) & (code <= Y * ROOM))
             def _():
-                r = code - 1
-                start = (r & 31) * BLK if room == 1 else ((r & 31) * SLOTS + (r >> 5)) * BLK
-                acc_ref[...] += dot(left[...], right_ref[tile_at(start), :])
-
-            @pl.when((code >= OWN) & (code < PLAIN))
+                acc_ref[...] += dot(left[...], right_ref[tile_at((code - 1) * BLK), :])
+
+            @pl.when(code >= OWN)
             def _():
-                acc_ref[...] += dot(left[...], square_ref[tile_at((code - OWN) * BLK), :])
-
-            @pl.when(code == PLAIN)
-            def _():
-                acc_ref[...] += dot(left[...], square_ref[TILES + o * BLK : TILES + (o + 1) * BLK, :])
+                start = jnp.where(code == PLAIN, TILES + o * BLK, (code - OWN) * BLK)
+                acc_ref[...] += dot(left[...], near_ref[tile_at(start), :])
 
         value = 1.5 * own_ref[part, :].astype(F32) - 0.5 * acc_ref[...]
         out_ref[:, part] = jnp.where(blocks[0, o] >= 0, value, 0.0).astype(BF16)
@@ -383,40 +397,32 @@
             pltpu.VMEM((128, 128), F32), pltpu.VMEM((128, 128), F32),
             pltpu.VMEM((NB, SLOTS_ROW * 128), BF16), pltpu.VMEM((SLOTS_ROW * 128, NB), BF16),
             pltpu.VMEM((32, 128), F32), pltpu.VMEM((32, 128), F32),
+            pltpu.VMEM((32, 128), F32), pltpu.VMEM((32, 128), F32),
             pltpu.SMEM((TERMS + 8, 128), jnp.int32), pltpu.SemaphoreType.DMA,
         ],
         compiler_params=PARAMS, name="plan",
     )(blocks, heads, second.reshape(XC * PANEL, BLK))
     left = swap(zbuf, "zl").reshape(ZL * TILES, BLK)
-    square = pl.pallas_call(
+    square, near = pl.pallas_call(
         square_kernel,
-        out_shape=like(2 * TILES, BLK),
-        in_specs=[SMEM] + [VMEM] * 3, out_specs=VMEM,
+        out_shape=(like(ZH, TILES, BLK), like(2 * TILES, BLK)),
+        in_specs=[SMEM] + [VMEM] * 3, out_specs=(VMEM, VMEM),
         scratch_shapes=[pltpu.VMEM((BLK, BLK), F32)], compiler_params=PARAMS, name="square",
     )(lists, own, left, right)
+    square = swap(square, "zh").reshape(ZH * TILES, BLK)
     send = pl.pallas_call(
         send_kernel,
-        out_shape=like(N_ROW, BLK, BLK),
+        out_shape=like(Y, ROOM * BLK, BLK),
         in_specs=[SMEM, VMEM], out_specs=VMEM, compiler_params=PARAMS, name="send",
     )(lists, square)
-
-    def finish(room, squares, lists, blocks, own, left, square):
-        return pl.pallas_call(
-            lambda *refs: cube_kernel(room, *refs),
-            out_shape=(like(*x.shape), like(1, dtype=jnp.int32)),
-            in_specs=[SMEM, SMEM] + [VMEM] * 4, out_specs=(VMEM, SMEM),
-            scratch_shapes=[pltpu.VMEM((BLK, BLK), F32)], compiler_params=PARAMS, name="cube%d" % room,
-        )(lists, blocks, own, left, square, squares)
-
-
-    kept = (lists, blocks, own, left, square)
-    result, level = finish(1, swap(send, ROW).reshape(N_ROW * BLK, BLK), *kept)
-    result, level, x, kept = lax.optimization_barrier((result, level, x, kept))
-
-    def roomy():
-        return finish(SLOTS, swap(jnp.tile(kept[-1][:TILES], (N_ROW, 1)), ROW), *kept)[0]
-
-    return lax.switch(level[0], [lambda: result, roomy, lambda: general(x, kept[1])])
+    result, level = pl.pallas_call(
+        cube_kernel,
+        out_shape=(like(*x.shape), like(1, dtype=jnp.int32)),
+        in_specs=[SMEM, SMEM] + [VMEM] * 4, out_specs=(VMEM, SMEM),
+        scratch_shapes=[pltpu.VMEM((BLK, BLK), F32)], compiler_params=PARAMS, name="cube",
+    )(lists, blocks, own, left, near, swap(send, "y").reshape(Y * ROOM * BLK, BLK))
+    result, level, x, blocks = lax.optimization_barrier((result, level, x, blocks))
+    return lax.cond(level[0] > 0, lambda: general(x, blocks), lambda: result)
 
 
 def solution(mesh):

time: 145 us -> 147 us (1.014)
  blocking collectives: 113 us -> 115 us
    all_to_all x4 -> x5, blocking collectives: 99.4 us -> 101 us  [swap(): return lax.all_to_all(value, axes, 0, 0, tiled=True)]
where the time goes in v4:
time: 147 us; the launch traced here: 146 us
  blocking collectives  115 us (78%)
  between operations  14.1 us (10%)
  Pallas kernels  13.1 us (9%)
  local copies, waits for them, and re-layouts  2.36 us (2%)
    all_to_all x5, blocking collectives, swap(): return lax.all_to_all(value, axes, 0, 0, tiled=True)  101 us
    all_gather x1, blocking collectives, per_device(): lax.all_gather(jnp.concatenate([own, heads], axis=0), ('x', 'c'), axis=0)  13.5 us
    pallas_call x1, Pallas kernels, per_device(): pl.pallas_call(plan_kernel, out_shape=(like(ZL, TILES, BLK), like(TERMS +...  7.7 us
  transfers between devices with their start and end apart: 1, of which 0 were waited for; matrix products, arithmetic and copies ran while one was open for 1% of the time, Pallas kernels for 5%

profile of v4, /device:TPU:6, one launch (start us, length us, event | category | flops | bytes accessed | tf_op | source)
XLA Modules:
  0.0 145.6 jit_solution(10706289069743946767)
XLA Ops:
  6.5 0.0 copy-start.3
  6.5 0.0 copy-start.2
  6.5 0.0 all-gather.14.cloned.1.call-start
  6.5 1.0 pack.1
  7.6 28.0 %all_to_all.26 = bf16[3,400,128]{2,1,0:T(8,128)(2,1)} all-to-all(bf16[3,400,128]{2,1,0:T(8,128)(2,1)S(1)} %get-tuple-element.28), channel_id=1, replica_groups=mesh['zh'=3,'y'=8,'zl'=4,'x'=4,'c'=2] {'zh'}, dimensions={0} | all-to-all | bytes 614400 | tf_op jit(solution)/shard_map/all_to_all | solution.py:372
  35.6 0.0 all-gather.14.cloned.1.call-update
  35.6 0.7 slice_reduce_fusion.3
  36.3 13.5 %all-gather.second_ref = bf16[3200,128]{1,0:T(8,128)(2,1)S(1)} all-gather(bf16[400,128]{1,0:T(8,128)(2,1)S(1)} %pad_maximum_fusion), channel_id=2, replica_groups=mesh['zh'=3,'y'=8,'zl'=4,'x'=4,'c'=2] {'x','c'}, dimensions={0}, use_global_device_ids=true | all-gather | bytes 921600 | tf_op jit(solution)/shard_map/all_gather | solution.py:388
  49.9 22.0 %all_to_all.27 = bf16[32,16,128]{2,1,0:T(8,128)(2,1)S(1)} all-to-all(bf16[32,16,128]{2,1,0:T(8,128)(2,1)S(1)} %broadcast_in_dim.43), channel_id=1, replica_groups=mesh['zh'=3,'y'=8,'zl'=4,'x'=4,'c'=2] {'y','zl'}, dimensions={0} | all-to-all | bytes 262144 | tf_op jit(solution)/shard_map/all_to_all | solution.py:372
  71.9 7.7 %plan.1 = (bf16[4,384,128]{2,1,0:T(8,128)(2,1)S(1)}, s32[24,128]{1,0:T(8,128)S(1)}) custom-call(s32[2,3]{1,0:T(2,128)} %blocks.5, bf16[8,64,128]{2,1,0:T(8,128)(2,1)S(1)} %bitcast.92, bf16[3200,128]{1,0:T(8,128)(2,1)S(1)} %all-gather.second_ref), custom_call_target="tpu_custom_call" | custom-call | tf_op jit(solution)/shard_map/plan/pallas_call | solution.py:392
  79.7 14.0 %all_to_all.28 = bf16[4,384,128]{2,1,0:T(8,128)(2,1)S(1)} all-to-all(bf16[4,384,128]{2,1,0:T(8,128)(2,1)S(1)} %get-tuple-element.30), channel_id=1, replica_groups=mesh['zh'=3,'y'=8,'zl'=4,'x'=4,'c'=2] {'zl'}, dimensions={0} | all-to-all | bytes 786432 | tf_op jit(solution)/shard_map/all_to_all | solution.py:372
  93.6 0.0 all-gather.14.cloned.1.call-done.right_ref
  93.6 0.0 copy-start
  93.6 1.7 %copy-done = bf16[9600,128]{1,0:T(8,128)(2,1)S(1)} copy-done((bf16[9600,128]{1,0:T(8,128)(2,1)S(1)}, bf16[9600,128]{1,0:T(8,128)(2,1)}, u32[]{:S(2)}) %copy-start) | copy-done | bytes 2457624
  95.3 1.4 square.1
  96.8 17.1 %all_to_all.29 = bf16[3,384,128]{2,1,0:T(8,128)(2,1)S(1)} all-to-all(bf16[3,384,128]{2,1,0:T(8,128)(2,1)S(1)} %get-tuple-element.32), channel_id=1, replica_groups=mesh['zh'=3,'y'=8,'zl'=4,'x'=4,'c'=2] {'zh'}, dimensions={0} | all-to-all | bytes 589824 | tf_op jit(solution)/shard_map/all_to_all | solution.py:372
  113.9 0.9 send.1
  114.7 20.4 %all_to_all.30 = bf16[8,256,128]{2,1,0:T(8,128)(2,1)S(1)} all-to-all(bf16[8,256,128]{2,1,0:T(8,128)(2,1)S(1)} %send.1), channel_id=1, replica_groups=mesh['zh'=3,'y'=8,'zl'=4,'x'=4,'c'=2] {'y'}, dimensions={0} | all-to-all | bytes 1048576 | tf_op jit(solution)/shard_map/all_to_all | solution.py:372
  135.1 0.0 copy-done.3
  135.1 2.1 %cube.1 = (bf16[128,384]{1,0:T(8,128)(2,1)S(1)}, s32[1]{0:T(128)}) custom-call(s32[24,128]{1,0:T(8,128)S(1)} %get-tuple-element.29.lists, s32[2,3]{1,0:T(2,128)S(1)} %copy-done.3, bf16[384,128]{1,0:T(8,128)(2,1)S(1)} %get-tuple-element.27.own_ref, bf16[1536,128]{1,0:T(8,128)(2,1)S(1)} %bitcast.88, bf16[768,128]{1,0:T(8,128)(2,1)S(1)} %get-tuple-element.31.near_ref, ...), custom_call_target="tpu_custom_call" | custom-call | tf_op jit(solution)/shard_map/cube/pallas_call | solution.py:418
  137.8 0.0 copy-done.2
  137.9 0.2 conditional.1
  138.1 0.0 copy-start.4
  138.1 0.6 copy-done.4
  (3 shorter events, 0.0 us)
Async XLA Ops:
  6.5 128.6 %copy-start.3 = (s32[2,3]{1,0:T(2,128)S(1)}, s32[2,3]{1,0:T(2,128)}, u32[]{:S(2)}) copy-start(s32[2,3]{1,0:T(2,128)} %blocks.5) | copy-start | bytes 76
  6.5 131.3 %copy-start.2 = (bf16[128,384]{1,0:T(8,128)(2,1)S(1)}, bf16[128,384]{1,0:T(8,128)(2,1)}, u32[]{:S(2)}) copy-start(bf16[128,384]{1,0:T(8,128)(2,1)} %x_ref.1) | copy-start | bytes 294916
  6.5 87.1 %all-gather.14.cloned.1.call-start = ((), (), s32[]{:S(2)}) async-start(), calls=%async_computation.8 | async-start | bytes 2764800 | tf_op jit(solution)/shard_map/all_gather | solution.py:386
  93.6 1.7 %copy-start = (bf16[9600,128]{1,0:T(8,128)(2,1)S(1)}, bf16[9600,128]{1,0:T(8,128)(2,1)}, u32[]{:S(2)}) copy-start(bf16[9600,128]{1,0:T(8,128)(2,1)} %all-gather.14.cloned.1.call-done.right_ref) | copy-start | bytes 7372804
  138.1 0.6 copy-start.4
Sparse Core Ops, SparseCore 0:
  35.7 46.6 all-gather.13

commit v5 on v4

--- a/solution.py
+++ b/solution.py
@@ -130,9 +130,20 @@
         out_ref[z, TILES:, :] = head
 
 
-def plan_kernel(
-    blocks, g_ref, second_ref, zbuf_ref, list_ref,
-    gij_ref, gt_ref, ohi_ref, ohj_ref, dy_ref, ry_ref, dl_ref, rl_ref, list_smem, sem,
+def row_tiles(gij_ref, p, lane):
+    li = jnp.full((1, 128), -1.0, F32)
+    lk = jnp.full((1, 128), -1.0, F32)
+    for z in range(ZL):
+        here = (lane >> 5 == z) & ((lane & 31) < SLOTS_ROW)
+        mine = jnp.broadcast_to(gij_ref[pl.ds(z * 32 + p, 1), :], (8, 128))
+        li = jnp.where(here, (pltpu.roll(mine, z * 32, 1) if z else mine)[0:1], li)
+        lk = jnp.where(here, pltpu.roll(mine, (64 + z * 32) % 128, 1)[0:1], lk)
+    return li, lk
+
+
+def left_kernel(
+    g_ref, second_ref, zbuf_ref, gij_ref, adj_ref, dl_ref, rl_ref,
+    ohi_ref, ohj_ref, list_ref, list_smem, sem,
 ):
     zh, y, zl, u, p, q = place()
     told = g_ref[...].astype(F32)
@@ -146,23 +157,68 @@
     g = jnp.where(((row128 & 31) < N_ROW) & ((lane128 & 63) < SLOTS_ROW), g, -1.0)
     gij_ref[...] = g
     gt = g.T
-    gt_ref[...] = gt
     sub = iota((NB, 128), 0).astype(F32)
     wide = iota((128, NB), 1).astype(F32)
     for k in range(SLOTS_ROW):
         ohi_ref[:, k * 128 : (k + 1) * 128] = onehot(sub == gt[k : k + 1, :])
         ohj_ref[k * 128 : (k + 1) * 128, :] = onehot(wide == g[:, 64 + k : 65 + k])
-    adj = dot(ohi_ref[...], ohj_ref[...])
-    adj_b = adj.astype(BF16)
-    adj_tf = adj.T
-    adj_t = adj_tf.astype(BF16)
-    mutual = adj * adj_tf
+    adj_b = dot(ohi_ref[...], ohj_ref[...]).astype(BF16)
+    adj_ref[...] = adj_b
     lane = iota((1, 128), 1)
+    rows, lanes = iota((32, 128), 0), iota((32, 128), 1)
+    rows8, lanes8 = iota((8, 128), 0), iota((8, 128), 1)
+    in_col = onehot(col_of(iota((32, NB), 1)) == iota((32, NB), 0))
+
+    li, lk = row_tiles(gij_ref, p, lane)
+    stack = jnp.where(row128 == 0, li, lk).T
+    both = dot(onehot(wide == stack[:, 0:1]), adj_b) * dot(onehot(wide == stack[:, 1:2]), adj_b)
+    count = lax.dot_general(in_col, both.astype(BF16), (((1,), (1,)), ((), ())), preferred_element_type=F32)
+    owner = (lanes >> 5) * XC + (((lanes & 31) * 11) >> 5)
+    wanted = (count > 0.5) & (owner != rows) & ((lanes & 31) < SLOTS_ROW)
+    wanted = jnp.where(wanted, 1.0, 0.0)
+    dl_ref[...] = wanted
+    rl_ref[...] = dot(wanted.astype(BF16), onehot((row128 < lane128) & ((row128 >> 5) == (lane128 >> 5))))
+    send_d = jnp.zeros((8, 128), F32)
+    send_r = jnp.zeros((8, 128), F32)
+    for z in range(ZL):
+        send_d = jnp.where(rows8 == z, dl_ref[pl.ds(z * XC + u, 1), :], send_d)
+        send_r = jnp.where(rows8 == z, rl_ref[pl.ds(z * XC + u, 1), :], send_r)
+    zlist = jnp.zeros((8, 128), F32)
+    for c in range(SLOTS):
+        hit = (send_d > 0.5) & (send_r == float(c)) & ((lanes8 >> 5) == zl)
+        code = jnp.sum(jnp.where(hit, ((lanes8 & 31) + 1).astype(F32), 0.0), axis=1, keepdims=True)
+        zlist = jnp.where(lanes8 == c, code, zlist)
+
+    list_ref[...] = zlist.astype(jnp.int32)
+    copy = pltpu.make_async_copy(list_ref, list_smem, sem)
+    copy.start()
+    copy.wait()
+    for d in range(ZL):
+        for c in range(SLOTS):
+            code = list_smem[d, c]
+
+            @pl.when(code > 0)
+            def _():
+                k = code - 1
+                src_u = (k * 11) >> 5
+                start = pl.multiple_of(src_u * PANEL + (k - src_u * SLOTS) * BLK, 16)
+                zbuf_ref[d, c * BLK : (c + 1) * BLK, :] = second_ref[pl.ds(start, BLK), :]
+
+
+def term_kernel(
+    blocks, gij_ref, adj_ref, dl_ref, rl_ref, list_ref, gt_ref, dy_ref, ry_ref,
+):
+    zh, y, zl, u, p, q = place()
+    gt_ref[...] = gij_ref[...].T
+    row128, lane128 = iota((128, 128), 0), iota((128, 128), 1)
+    sub = iota((NB, 128), 0).astype(F32)
+    adj_b = adj_ref[...]
+    adj = adj_b.astype(F32)
+    mutual = adj * adj.T
+    lane = iota((1, 128), 1)
+    lanes = iota((32, 128), 1)
     rows = iota((32, 128), 0)
-    lanes = iota((32, 128), 1)
-    number = iota((32, NB), 1)
-    in_row = onehot(row_of(number) == iota((32, NB), 0))
-    in_col = onehot(col_of(number) == iota((32, NB), 0))
+    in_row = onehot(row_of(iota((32, NB), 1)) == iota((32, NB), 0))
     in_col_t = onehot(col_of(iota((NB, 32), 0)) == iota((NB, 32), 1))
 
     ci = jnp.full((1, 128), -1.0, F32)
@@ -193,29 +249,7 @@
         code = jnp.sum(jnp.where(hit, (lanes8 + 1).astype(F32), 0.0), axis=1, keepdims=True)
         ylist = jnp.where(lanes8 == c, code, ylist)
 
-    li = jnp.full((1, 128), -1.0, F32)
-    lk = jnp.full((1, 128), -1.0, F32)
-    for z in range(ZL):
-        here = (lane >> 5 == z) & ((lane & 31) < SLOTS_ROW)
-        mine = jnp.broadcast_to(gij_ref[pl.ds(z * 32 + p, 1), :], (8, 128))
-        li = jnp.where(here, (pltpu.roll(mine, z * 32, 1) if z else mine)[0:1], li)
-        lk = jnp.where(here, pltpu.roll(mine, (64 + z * 32) % 128, 1)[0:1], lk)
-    both = dot(adj_t, onehot(sub == li)) * dot(adj_t, onehot(sub == lk))
-    owner = (lanes >> 5) * XC + (((lanes & 31) * 11) >> 5)
-    wanted = (dot(in_col, both.astype(BF16)) > 0.5) & (owner != rows) & ((lanes & 31) < SLOTS_ROW)
-    wanted = jnp.where(wanted, 1.0, 0.0)
-    dl_ref[...] = wanted
-    rl_ref[...] = dot(wanted.astype(BF16), onehot((row128 < lane128) & ((row128 >> 5) == (lane128 >> 5))))
-    send_d = jnp.zeros((8, 128), F32)
-    send_r = jnp.zeros((8, 128), F32)
-    for z in range(ZL):
-        send_d = jnp.where(rows8 == z, dl_ref[pl.ds(z * XC + u, 1), :], send_d)
-        send_r = jnp.where(rows8 == z, rl_ref[pl.ds(z * XC + u, 1), :], send_r)
-    zlist = jnp.zeros((8, 128), F32)
-    for c in range(SLOTS):
-        hit = (send_d > 0.5) & (send_r == float(c)) & ((lanes8 >> 5) == zl)
-        code = jnp.sum(jnp.where(hit, ((lanes8 & 31) + 1).astype(F32), 0.0), axis=1, keepdims=True)
-        zlist = jnp.where(lanes8 == c, code, zlist)
+    li, lk = row_tiles(gij_ref, p, lane)
 
     right = jnp.where(ci >= 0.0, (lane + 1).astype(F32), 0.0)
     got_d, got_r = dy_ref[pl.ds(p, 1), :], ry_ref[pl.ds(p, 1), :]
@@ -274,24 +308,11 @@
         per_dev(dot(jnp.where(((k_row >> bit) & 1) == 1, moving, 0.0).astype(BF16), target)) for bit in (0, 1, 2)
     ]
     over = jnp.maximum(over, fullest(total, parts, ROOM))
-    zlist = jnp.where((rows8 == 7) & (lanes8 == 0), over, zlist)
+    level = jnp.where((rows8 == 7) & (lanes8 == 0), over, 0.0)
 
     list_ref[0:ZLIST, :] = ylist.astype(jnp.int32)
-    list_ref[ZLIST:TERMS, :] = zlist.astype(jnp.int32)
+    list_ref[ZLIST:TERMS, :] = level.astype(jnp.int32)
     list_ref[TERMS:, :] = terms.astype(jnp.int32)
-    copy = pltpu.make_async_copy(list_ref, list_smem, sem)
-    copy.start()
-    copy.wait()
-    for d in range(ZL):
-        for c in range(SLOTS):
-            code = list_smem[ZLIST + d, c]
-
-            @pl.when(code > 0)
-            def _():
-                k = code - 1
-                src_u = (k * 11) >> 5
-                start = pl.multiple_of(src_u * PANEL + (k - src_u * SLOTS) * BLK, 16)
-                zbuf_ref[d, c * BLK : (c + 1) * BLK, :] = second_ref[pl.ds(start, BLK), :]
 
 
 def tile_at(start):
@@ -389,20 +410,28 @@
     heads = jnp.sum(second[:, TILES:].astype(F32), axis=0).astype(BF16)
     heads = jnp.broadcast_to(heads[None], (Y * ZL, HEAD, 128)).reshape(Y * ZL * HEAD, 128)
     heads = swap(heads, ("y", "zl")).reshape(Y, ZL * HEAD, 128)
-    zbuf, lists = pl.pallas_call(
-        plan_kernel,
-        out_shape=(like(ZL, TILES, BLK), like(TERMS + 8, 128, dtype=jnp.int32)),
-        in_specs=[SMEM, VMEM, VMEM], out_specs=(VMEM, VMEM),
+    zbuf, known, adjacent, wanted, ranks = pl.pallas_call(
+        left_kernel,
+        out_shape=(
+            like(ZL, TILES, BLK), like(128, 128, dtype=F32), like(NB, NB),
+            like(32, 128, dtype=F32), like(32, 128, dtype=F32),
+        ),
+        in_specs=[VMEM, VMEM], out_specs=(VMEM,) * 5,
         scratch_shapes=[
-            pltpu.VMEM((128, 128), F32), pltpu.VMEM((128, 128), F32),
             pltpu.VMEM((NB, SLOTS_ROW * 128), BF16), pltpu.VMEM((SLOTS_ROW * 128, NB), BF16),
-            pltpu.VMEM((32, 128), F32), pltpu.VMEM((32, 128), F32),
-            pltpu.VMEM((32, 128), F32), pltpu.VMEM((32, 128), F32),
-            pltpu.SMEM((TERMS + 8, 128), jnp.int32), pltpu.SemaphoreType.DMA,
+            pltpu.VMEM((8, 128), jnp.int32), pltpu.SMEM((8, 128), jnp.int32), pltpu.SemaphoreType.DMA,
         ],
-        compiler_params=PARAMS, name="plan",
-    )(blocks, heads, second.reshape(XC * PANEL, BLK))
+        compiler_params=PARAMS, name="left",
+    )(heads, second.reshape(XC * PANEL, BLK))
     left = swap(zbuf, "zl").reshape(ZL * TILES, BLK)
+    lists = pl.pallas_call(
+        term_kernel,
+        out_shape=like(TERMS + 8, 128, dtype=jnp.int32),
+        in_specs=[SMEM] + [VMEM] * 4, out_specs=VMEM,
+        scratch_shapes=[pltpu.VMEM((128, 128), F32), pltpu.VMEM((32, 128), F32), pltpu.VMEM((32, 128), F32)],
+        cost_estimate=pl.CostEstimate(flops=2_000_000_000, bytes_accessed=1_000_000, transcendentals=0),
+        compiler_params=PARAMS, name="term",
+    )(blocks, known, adjacent, wanted, ranks)
     square, near = pl.pallas_call(
         square_kernel,
         out_shape=(like(ZH, TILES, BLK), like(2 * TILES, BLK)),

time: 147 us -> 141 us (0.959)
  blocking collectives: 115 us -> 99.5 us
  waiting for transfers between devices: 0.02 us -> 6.11 us
  starting transfers between devices: 0.01 us -> 3.48 us
    all_to_all x5 -> x4, blocking collectives: 101 us -> 86 us  [swap(): return lax.all_to_all(value, axes, 0, 0, tiled=True)]
    all_to_all x0 -> x1, waiting for transfers between devices: none -> 6.09 us  [swap(): return lax.all_to_all(value, axes, 0, 0, tiled=True)]
    all_to_all x0 -> x1, starting transfers between devices: none -> 3.47 us  [swap(): return lax.all_to_all(value, axes, 0, 0, tiled=True)]
    pallas_call x1 -> x2, Pallas kernels: 7.7 us -> 8.75 us  [the longest x1 4.79 us: per_device(): pl.pallas_call(term_kernel, out_shape=like(TERMS + 8, 128, dtype=jnp.int3...]
  transfers between devices with their start and end apart: 1 -> 2, of which waited for: 0 -> 1; matrix products, arithmetic and copies ran while one was open for 1% -> 1% of each run, Pallas kernels for 5% -> 6%
where the time goes in v5:
time: 141 us; the launch traced here: 140 us
  blocking collectives  99.5 us (71%)
  between operations  14.1 us (10%)
  Pallas kernels  13.7 us (10%)
  waiting for transfers between devices  6.11 us (4%)
  starting transfers between devices  3.48 us (2%)
  local copies, waits for them, and re-layouts  2.36 us (2%)
    all_to_all x4, blocking collectives, swap(): return lax.all_to_all(value, axes, 0, 0, tiled=True)  86 us
    all_gather x1, blocking collectives, per_device(): lax.all_gather(jnp.concatenate([own, heads], axis=0), ('x', 'c'), axis=0)  13.5 us
    all_to_all x1, waiting for transfers between devices, swap(): return lax.all_to_all(value, axes, 0, 0, tiled=True)  6.09 us
    pallas_call x1, Pallas kernels, per_device(): pl.pallas_call(term_kernel, out_shape=like(TERMS + 8, 128, dtype=jnp.int3...  4.79 us
    pallas_call x1, Pallas kernels, per_device(): pl.pallas_call(left_kernel, out_shape=(like(ZL, TILES, BLK), like(128, 12...  3.95 us
    all_to_all x1, starting transfers between devices, swap(): return lax.all_to_all(value, axes, 0, 0, tiled=True)  3.47 us
  transfers between devices with their start and end apart: 2, of which 1 were waited for; matrix products, arithmetic and copies ran while one was open for 1% of the time, Pallas kernels for 6%

profile of v5, /device:TPU:6, one launch (start us, length us, event | category | flops | bytes accessed | tf_op | source)
XLA Modules:
  0.0 140.3 jit_solution(16407459288100149249)
XLA Ops:
  6.5 0.0 copy-start.3
  6.5 0.0 copy-start.2
  6.5 0.0 all-gather.14.cloned.1.call-start
  6.5 1.0 pack.1
  7.6 28.0 %all_to_all.26 = bf16[3,400,128]{2,1,0:T(8,128)(2,1)} all-to-all(bf16[3,400,128]{2,1,0:T(8,128)(2,1)S(1)} %get-tuple-element.31), channel_id=1, replica_groups=mesh['zh'=3,'y'=8,'zl'=4,'x'=4,'c'=2] {'zh'}, dimensions={0} | all-to-all | bytes 614400 | tf_op jit(solution)/shard_map/all_to_all | solution.py:393
  35.6 0.0 all-gather.14.cloned.1.call-update
  35.6 0.7 slice_reduce_fusion.3
  36.3 13.5 %all-gather.second_ref = bf16[3200,128]{1,0:T(8,128)(2,1)S(1)} all-gather(bf16[400,128]{1,0:T(8,128)(2,1)S(1)} %pad_maximum_fusion), channel_id=2, replica_groups=mesh['zh'=3,'y'=8,'zl'=4,'x'=4,'c'=2] {'x','c'}, dimensions={0}, use_global_device_ids=true | all-gather | bytes 921600 | tf_op jit(solution)/shard_map/all_gather | solution.py:409
  49.9 22.0 %all_to_all.27 = bf16[32,16,128]{2,1,0:T(8,128)(2,1)S(1)} all-to-all(bf16[32,16,128]{2,1,0:T(8,128)(2,1)S(1)} %broadcast_in_dim.43), channel_id=1, replica_groups=mesh['zh'=3,'y'=8,'zl'=4,'x'=4,'c'=2] {'y','zl'}, dimensions={0} | all-to-all | bytes 262144 | tf_op jit(solution)/shard_map/all_to_all | solution.py:393
  71.9 4.0 %left.1 = (bf16[4,384,128]{2,1,0:T(8,128)(2,1)}, f32[128,128]{1,0:T(8,128)S(1)}, bf16[384,384]{1,0:T(8,128)(2,1)S(1)}, f32[32,128]{1,0:T(8,128)S(1)}, f32[32,128]{1,0:T(8,128)S(1)}) custom-call(bf16[8,64,128]{2,1,0:T(8,128)(2,1)S(1)} %bitcast.92, bf16[3200,128]{1,0:T(8,128)(2,1)S(1)} %all-gather.second_ref), custom_call_target="tpu_custom_call" | custom-call | tf_op jit(solution)/shard_map/left/pallas_call | solution.py:413
  75.9 3.5 %all-to-all-start.2 = ((bf16[4,384,128]{2,1,0:T(8,128)(2,1)}), bf16[4,384,128]{2,1,0:T(8,128)(2,1)S(1)}, u32[]{:S(2)}, u32[]{:S(2)}) async-start(bf16[4,384,128]{2,1,0:T(8,128)(2,1)} %get-tuple-element.36), calls=%async_computation.2 | async-start | bytes 786432 | tf_op jit(solution)/shard_map/all_to_all | solution.py:393
  79.4 4.8 %term.1.lists = s32[24,128]{1,0:T(8,128)S(1)} custom-call(s32[2,3]{1,0:T(2,128)} %blocks.5, f32[128,128]{1,0:T(8,128)S(1)} %get-tuple-element.32.gij_ref, bf16[384,384]{1,0:T(8,128)(2,1)S(1)} %get-tuple-element.33.adj_ref, f32[32,128]{1,0:T(8,128)S(1)} %get-tuple-element.34.dl_ref, f32[32,128]{1,0:T(8,128)S(1)} %get-tuple-element.35.rl_ref), custom_call_target="tpu_custom_call" | custom-call | flops 2000000000 | bytes 1000000 | tf_op jit(solution)/shard_map/term/pallas_call | solution.py:427
  84.2 6.1 %all-to-all-done.2 = bf16[4,384,128]{2,1,0:T(8,128)(2,1)S(1)} async-done(((bf16[4,384,128]{2,1,0:T(8,128)(2,1)}), bf16[4,384,128]{2,1,0:T(8,128)(2,1)S(1)}, u32[]{:S(2)}, u32[]{:S(2)}) %all-to-all-start.2) | async-done | bytes 393248 | tf_op jit(solution)/shard_map/all_to_all | solution.py:393
  90.3 0.0 all-gather.14.cloned.1.call-done.right_ref
  90.3 0.0 copy-start
  90.3 1.7 %copy-done = bf16[9600,128]{1,0:T(8,128)(2,1)S(1)} copy-done((bf16[9600,128]{1,0:T(8,128)(2,1)S(1)}, bf16[9600,128]{1,0:T(8,128)(2,1)}, u32[]{:S(2)}) %copy-start) | copy-done | bytes 2457624
  92.0 1.1 square.1
  93.1 16.2 %all_to_all.28 = bf16[3,384,128]{2,1,0:T(8,128)(2,1)S(1)} all-to-all(bf16[3,384,128]{2,1,0:T(8,128)(2,1)S(1)} %get-tuple-element.38), channel_id=1, replica_groups=mesh['zh'=3,'y'=8,'zl'=4,'x'=4,'c'=2] {'zh'}, dimensions={0} | all-to-all | bytes 589824 | tf_op jit(solution)/shard_map/all_to_all | solution.py:393
  109.3 0.9 send.1
  110.2 19.8 %all_to_all.29 = bf16[8,256,128]{2,1,0:T(8,128)(2,1)S(1)} all-to-all(bf16[8,256,128]{2,1,0:T(8,128)(2,1)S(1)} %send.1), channel_id=1, replica_groups=mesh['zh'=3,'y'=8,'zl'=4,'x'=4,'c'=2] {'y'}, dimensions={0} | all-to-all | bytes 1048576 | tf_op jit(solution)/shard_map/all_to_all | solution.py:393
  130.0 0.0 copy-done.3
  130.0 1.9 %cube.1 = (bf16[128,384]{1,0:T(8,128)(2,1)S(1)}, s32[1]{0:T(128)}) custom-call(s32[24,128]{1,0:T(8,128)S(1)} %term.1.lists, s32[2,3]{1,0:T(2,128)S(1)} %copy-done.3, bf16[384,128]{1,0:T(8,128)(2,1)S(1)} %get-tuple-element.30.own_ref, bf16[1536,128]{1,0:T(8,128)(2,1)S(1)} %bitcast.88, bf16[768,128]{1,0:T(8,128)(2,1)S(1)} %get-tuple-element.37.near_ref, ...), custom_call_target="tpu_custom_call" | custom-call | tf_op jit(solution)/shard_map/cube/pallas_call | solution.py:447
  132.5 0.0 copy-done.2
  132.5 0.2 conditional.1
  132.8 0.0 copy-start.4
  132.8 0.6 copy-done.4
  (3 shorter events, 0.0 us)
Async XLA Ops:
  6.5 123.4 %copy-start.3 = (s32[2,3]{1,0:T(2,128)S(1)}, s32[2,3]{1,0:T(2,128)}, u32[]{:S(2)}) copy-start(s32[2,3]{1,0:T(2,128)} %blocks.5) | copy-start | bytes 76
  6.5 126.0 %copy-start.2 = (bf16[128,384]{1,0:T(8,128)(2,1)S(1)}, bf16[128,384]{1,0:T(8,128)(2,1)}, u32[]{:S(2)}) copy-start(bf16[128,384]{1,0:T(8,128)(2,1)} %x_ref.1) | copy-start | bytes 294916
  6.5 83.7 %all-gather.14.cloned.1.call-start = ((), (), s32[]{:S(2)}) async-start(), calls=%async_computation.8 | async-start | bytes 2764800 | tf_op jit(solution)/shard_map/all_gather | solution.py:407
  75.9 14.4 %all-to-all-start.2 = ((bf16[4,384,128]{2,1,0:T(8,128)(2,1)}), bf16[4,384,128]{2,1,0:T(8,128)(2,1)S(1)}, u32[]{:S(2)}, u32[]{:S(2)}) async-start(bf16[4,384,128]{2,1,0:T(8,128)(2,1)} %get-tuple-element.36), calls=%async_computation.2 | async-start | bytes 786432 | tf_op jit(solution)/shard_map/all_to_all | solution.py:393
  90.3 1.7 %copy-start = (bf16[9600,128]{1,0:T(8,128)(2,1)S(1)}, bf16[9600,128]{1,0:T(8,128)(2,1)}, u32[]{:S(2)}) copy-start(bf16[9600,128]{1,0:T(8,128)(2,1)} %all-gather.14.cloned.1.call-done.right_ref) | copy-start | bytes 7372804
  132.8 0.6 copy-start.4
Sparse Core Ops, SparseCore 0:
  35.7 46.6 all-gather.13

commit v6 on v5

--- a/solution.py
+++ b/solution.py
@@ -18,6 +18,7 @@
 LEFTS = ZL * SLOTS + SLOTS
 OWN, PLAIN = 128, 160
 ROOM = 2
+ZROOM = 2
 ZLIST, TERMS = 8, 16
 ROW = ("zh", "y")
 COL = ("zl", "x", "c")
@@ -214,7 +215,8 @@
     sub = iota((NB, 128), 0).astype(F32)
     adj_b = adj_ref[...]
     adj = adj_b.astype(F32)
-    mutual = adj * adj.T
+    adj_t = adj.T
+    mutual = adj * adj_t
     lane = iota((1, 128), 1)
     lanes = iota((32, 128), 1)
     rows = iota((32, 128), 0)
@@ -241,13 +243,24 @@
     ry_ref[...] = dot(wanted.astype(BF16), onehot((row128 < lane128) & ((row128 & 7) == (lane128 & 7))))
     lanes8 = iota((8, 128), 1)
     rows8 = iota((8, 128), 0)
+    plane_d = jnp.zeros((8, 128), F32)
+    for z in range(ZH):
+        plane = jnp.max(wanted[z * Y : (z + 1) * Y], axis=0, keepdims=True)
+        plane_d = jnp.where(rows8 == z, plane, plane_d)
+    plane_r = dot(plane_d.astype(BF16), onehot((row128 < lane128) & ((row128 & 31) == (lane128 & 31))))
+    place_z = jnp.sum(jnp.where(rows8 == zh, plane_r, 0.0), axis=0, keepdims=True)
+    place_z = place_z + (((lane & 31) >> 3) * ZROOM + 1).astype(F32)
     send_d = dy_ref[pl.ds(pl.multiple_of(zh * Y, 8), 8), :]
     send_r = ry_ref[pl.ds(pl.multiple_of(zh * Y, 8), 8), :]
     ylist = jnp.zeros((8, 128), F32)
     for c in range(ROOM):
         hit = (send_d > 0.5) & (send_r == float(c)) & ((lanes8 & 7) == y)
-        code = jnp.sum(jnp.where(hit, (lanes8 + 1).astype(F32), 0.0), axis=1, keepdims=True)
+        code = jnp.sum(jnp.where(hit, place_z, 0.0), axis=1, keepdims=True)
         ylist = jnp.where(lanes8 == c, code, ylist)
+    for c in range(ZROOM):
+        hit = (plane_d > 0.5) & (plane_r == float(c)) & ((lanes8 & 31) == p)
+        code = jnp.sum(jnp.where(hit, ((lanes8 >> 5) + 1).astype(F32), 0.0), axis=1, keepdims=True)
+        ylist = jnp.where(lanes8 == 8 + c, code, ylist)
 
     li, lk = row_tiles(gij_ref, p, lane)
 
@@ -308,6 +321,9 @@
         per_dev(dot(jnp.where(((k_row >> bit) & 1) == 1, moving, 0.0).astype(BF16), target)) for bit in (0, 1, 2)
     ]
     over = jnp.maximum(over, fullest(total, parts, ROOM))
+    asked = dot(jnp.where(i_row != k_row, adj_t, 0.0).astype(BF16), adj_b) * target.astype(F32)
+    asked = dot(dot(in_row, onehot(asked > 0.5)).astype(BF16), in_col_t)
+    over = jnp.maximum(over, fullest(asked, [], ZROOM))
     level = jnp.where((rows8 == 7) & (lanes8 == 0), over, 0.0)
 
     list_ref[0:ZLIST, :] = ylist.astype(jnp.int32)
@@ -345,8 +361,6 @@
 
         tile = acc_ref[...].astype(BF16)
         near_ref[part, :] = tile
-        for z in range(ZH):
-            out_ref[z, part, :] = tile
         code = lists[TERMS + o, 64]
 
         @pl.when(code > 0)
@@ -354,17 +368,23 @@
             tile = right_ref[tile_at(panel_start(code)), :]
             near_ref[TILES + o * BLK : TILES + (o + 1) * BLK, :] = dot(tile, tile).astype(BF16)
 
+    for z in range(ZH):
+        for c in range(ZROOM):
+            code = lists[z, 8 + c]
+
+            @pl.when((code > 0) & (code <= SLOTS))
+            def _():
+                out_ref[z, c * BLK : (c + 1) * BLK, :] = near_ref[tile_at((code - 1) * BLK), :]
+
 
 def send_kernel(lists, square_ref, send_ref):
     for d in range(Y):
         for c in range(ROOM):
             code = lists[d, c]
 
-            @pl.when(code > 0)
-            def _():
-                r = code - 1
-                start = ((r >> 3) & 3) * TILES + (r >> 5) * BLK
-                send_ref[d, c * BLK : (c + 1) * BLK, :] = square_ref[tile_at(start), :]
+            @pl.when((code > 0) & (code <= ZH * ZROOM))
+            def _():
+                send_ref[d, c * BLK : (c + 1) * BLK, :] = square_ref[tile_at((code - 1) * BLK), :]
 
 
 def cube_kernel(lists, blocks, own_ref, left_ref, near_ref, right_ref, out_ref, level_ref, acc_ref):
@@ -434,11 +454,11 @@
     )(blocks, known, adjacent, wanted, ranks)
     square, near = pl.pallas_call(
         square_kernel,
-        out_shape=(like(ZH, TILES, BLK), like(2 * TILES, BLK)),
+        out_shape=(like(ZH, ZROOM * BLK, BLK), like(2 * TILES, BLK)),
         in_specs=[SMEM] + [VMEM] * 3, out_specs=(VMEM, VMEM),
         scratch_shapes=[pltpu.VMEM((BLK, BLK), F32)], compiler_params=PARAMS, name="square",
     )(lists, own, left, right)
-    square = swap(square, "zh").reshape(ZH * TILES, BLK)
+    square = swap(square, "zh").reshape(ZH * ZROOM * BLK, BLK)
     send = pl.pallas_call(
         send_kernel,
         out_shape=like(Y, ROOM * BLK, BLK),

time: 141 us -> 136 us (0.965)
  blocking collectives: 99.5 us -> 94.1 us
  Pallas kernels: 13.7 us -> 15.3 us
    all_to_all x4, blocking collectives: 86 us -> 80.5 us  [swap(): return lax.all_to_all(value, axes, 0, 0, tiled=True)]
  transfers between devices with their start and end apart: 2 -> 2, of which waited for: 1 -> 1; matrix products, arithmetic and copies ran while one was open for 1% -> 1% of each run, Pallas kernels for 6% -> 7%
where the time goes in v6:
time: 136 us
  blocking collectives  94.1 us (69%)
  Pallas kernels  15.3 us (11%)
  between operations  14.1 us (10%)
  waiting for transfers between devices  5.49 us (4%)
  starting transfers between devices  3.48 us (3%)
  local copies, waits for them, and re-layouts  2.36 us (2%)
    all_to_all x4, blocking collectives, swap(): return lax.all_to_all(value, axes, 0, 0, tiled=True)  80.5 us
    all_gather x1, blocking collectives, per_device(): lax.all_gather(jnp.concatenate([own, heads], axis=0), ('x', 'c'), axis=0)  13.5 us
    all_to_all x1, waiting for transfers between devices, swap(): return lax.all_to_all(value, axes, 0, 0, tiled=True)  5.47 us
    pallas_call x1, Pallas kernels, per_device(): pl.pallas_call(term_kernel, out_shape=like(TERMS + 8, 128, dtype=jnp.int3...  5.41 us
    pallas_call x1, Pallas kernels, per_device(): pl.pallas_call(left_kernel, out_shape=(like(ZL, TILES, BLK), like(128, 12...  3.94 us
    all_to_all x1, starting transfers between devices, swap(): return lax.all_to_all(value, axes, 0, 0, tiled=True)  3.47 us
  transfers between devices with their start and end apart: 2, of which 1 were waited for; matrix products, arithmetic and copies ran while one was open for 1% of the time, Pallas kernels for 7%

profile of v6, /device:TPU:6, one launch (start us, length us, event | category | flops | bytes accessed | tf_op | source)
XLA Modules:
  0.0 135.7 jit_solution(18005474225678965147)
XLA Ops:
  6.5 0.0 copy-start.3
  6.5 0.0 copy-start.2
  6.5 0.0 all-gather.14.cloned.1.call-start
  6.5 1.0 pack.1
  7.6 28.0 %all_to_all.26 = bf16[3,400,128]{2,1,0:T(8,128)(2,1)} all-to-all(bf16[3,400,128]{2,1,0:T(8,128)(2,1)S(1)} %get-tuple-element.31), channel_id=1, replica_groups=mesh['zh'=3,'y'=8,'zl'=4,'x'=4,'c'=2] {'zh'}, dimensions={0} | all-to-all | bytes 614400 | tf_op jit(solution)/shard_map/all_to_all | solution.py:413
  35.6 0.0 all-gather.14.cloned.1.call-update
  35.6 0.7 slice_reduce_fusion.3
  36.3 13.5 %all-gather.second_ref = bf16[3200,128]{1,0:T(8,128)(2,1)S(1)} all-gather(bf16[400,128]{1,0:T(8,128)(2,1)S(1)} %pad_maximum_fusion), channel_id=2, replica_groups=mesh['zh'=3,'y'=8,'zl'=4,'x'=4,'c'=2] {'x','c'}, dimensions={0}, use_global_device_ids=true | all-gather | bytes 921600 | tf_op jit(solution)/shard_map/all_gather | solution.py:429
  49.9 22.0 %all_to_all.27 = bf16[32,16,128]{2,1,0:T(8,128)(2,1)S(1)} all-to-all(bf16[32,16,128]{2,1,0:T(8,128)(2,1)S(1)} %broadcast_in_dim.43), channel_id=1, replica_groups=mesh['zh'=3,'y'=8,'zl'=4,'x'=4,'c'=2] {'y','zl'}, dimensions={0} | all-to-all | bytes 262144 | tf_op jit(solution)/shard_map/all_to_all | solution.py:413
  71.9 3.9 %left.1 = (bf16[4,384,128]{2,1,0:T(8,128)(2,1)}, f32[128,128]{1,0:T(8,128)S(1)}, bf16[384,384]{1,0:T(8,128)(2,1)S(1)}, f32[32,128]{1,0:T(8,128)S(1)}, f32[32,128]{1,0:T(8,128)S(1)}) custom-call(bf16[8,64,128]{2,1,0:T(8,128)(2,1)S(1)} %bitcast.92, bf16[3200,128]{1,0:T(8,128)(2,1)S(1)} %all-gather.second_ref), custom_call_target="tpu_custom_call" | custom-call | tf_op jit(solution)/shard_map/left/pallas_call | solution.py:433
  75.9 3.5 %all-to-all-start.2 = ((bf16[4,384,128]{2,1,0:T(8,128)(2,1)}), bf16[4,384,128]{2,1,0:T(8,128)(2,1)S(1)}, u32[]{:S(2)}, u32[]{:S(2)}) async-start(bf16[4,384,128]{2,1,0:T(8,128)(2,1)} %get-tuple-element.36), calls=%async_computation.2 | async-start | bytes 786432 | tf_op jit(solution)/shard_map/all_to_all | solution.py:413
  79.4 5.4 %term.1.lists = s32[24,128]{1,0:T(8,128)S(1)} custom-call(s32[2,3]{1,0:T(2,128)} %blocks.5, f32[128,128]{1,0:T(8,128)S(1)} %get-tuple-element.32.gij_ref, bf16[384,384]{1,0:T(8,128)(2,1)S(1)} %get-tuple-element.33.adj_ref, f32[32,128]{1,0:T(8,128)S(1)} %get-tuple-element.34.dl_ref, f32[32,128]{1,0:T(8,128)S(1)} %get-tuple-element.35.rl_ref), custom_call_target="tpu_custom_call" | custom-call | flops 2000000000 | bytes 1000000 | tf_op jit(solution)/shard_map/term/pallas_call | solution.py:447
  84.8 5.5 %all-to-all-done.2 = bf16[4,384,128]{2,1,0:T(8,128)(2,1)S(1)} async-done(((bf16[4,384,128]{2,1,0:T(8,128)(2,1)}), bf16[4,384,128]{2,1,0:T(8,128)(2,1)S(1)}, u32[]{:S(2)}, u32[]{:S(2)}) %all-to-all-start.2) | async-done | bytes 393248 | tf_op jit(solution)/shard_map/all_to_all | solution.py:413
  90.3 0.0 all-gather.14.cloned.1.call-done.right_ref
  90.3 0.0 copy-start
  90.3 1.7 %copy-done = bf16[9600,128]{1,0:T(8,128)(2,1)S(1)} copy-done((bf16[9600,128]{1,0:T(8,128)(2,1)S(1)}, bf16[9600,128]{1,0:T(8,128)(2,1)}, u32[]{:S(2)}) %copy-start) | copy-done | bytes 2457624
  92.0 1.8 %square.1 = (bf16[3,256,128]{2,1,0:T(8,128)(2,1)S(1)}, bf16[768,128]{1,0:T(8,128)(2,1)S(1)}) custom-call(s32[24,128]{1,0:T(8,128)S(1)} %term.1.lists, bf16[384,128]{1,0:T(8,128)(2,1)S(1)} %get-tuple-element.30.own_ref, bf16[1536,128]{1,0:T(8,128)(2,1)S(1)} %bitcast.87, bf16[9600,128]{1,0:T(8,128)(2,1)S(1)} %copy-done), custom_call_target="tpu_custom_call" | custom-call | tf_op jit(solution)/shard_map/square/pallas_call | solution.py:455
  93.7 14.4 %all_to_all.28 = bf16[3,256,128]{2,1,0:T(8,128)(2,1)S(1)} all-to-all(bf16[3,256,128]{2,1,0:T(8,128)(2,1)S(1)} %get-tuple-element.38), channel_id=1, replica_groups=mesh['zh'=3,'y'=8,'zl'=4,'x'=4,'c'=2] {'zh'}, dimensions={0} | all-to-all | bytes 393216 | tf_op jit(solution)/shard_map/all_to_all | solution.py:413
  108.2 0.9 send.1
  109.0 16.1 %all_to_all.29 = bf16[8,256,128]{2,1,0:T(8,128)(2,1)S(1)} all-to-all(bf16[8,256,128]{2,1,0:T(8,128)(2,1)S(1)} %send.1), channel_id=1, replica_groups=mesh['zh'=3,'y'=8,'zl'=4,'x'=4,'c'=2] {'y'}, dimensions={0} | all-to-all | bytes 1048576 | tf_op jit(solution)/shard_map/all_to_all | solution.py:413
  125.1 0.0 copy-done.3
  125.1 2.2 %cube.1 = (bf16[128,384]{1,0:T(8,128)(2,1)S(1)}, s32[1]{0:T(128)}) custom-call(s32[24,128]{1,0:T(8,128)S(1)} %term.1.lists, s32[2,3]{1,0:T(2,128)S(1)} %copy-done.3, bf16[384,128]{1,0:T(8,128)(2,1)S(1)} %get-tuple-element.30.own_ref, bf16[1536,128]{1,0:T(8,128)(2,1)S(1)} %bitcast.88, bf16[768,128]{1,0:T(8,128)(2,1)S(1)} %get-tuple-element.37.near_ref, ...), custom_call_target="tpu_custom_call" | custom-call | tf_op jit(solution)/shard_map/cube/pallas_call | solution.py:467
  128.0 0.0 copy-done.2
  128.0 0.2 conditional.1
  128.2 0.0 copy-start.4
  128.3 0.6 copy-done.4
  (3 shorter events, 0.0 us)
Async XLA Ops:
  6.5 118.6 %copy-start.3 = (s32[2,3]{1,0:T(2,128)S(1)}, s32[2,3]{1,0:T(2,128)}, u32[]{:S(2)}) copy-start(s32[2,3]{1,0:T(2,128)} %blocks.5) | copy-start | bytes 76
  6.5 121.5 %copy-start.2 = (bf16[128,384]{1,0:T(8,128)(2,1)S(1)}, bf16[128,384]{1,0:T(8,128)(2,1)}, u32[]{:S(2)}) copy-start(bf16[128,384]{1,0:T(8,128)(2,1)} %x_ref.1) | copy-start | bytes 294916
  6.5 83.7 %all-gather.14.cloned.1.call-start = ((), (), s32[]{:S(2)}) async-start(), calls=%async_computation.8 | async-start | bytes 2764800 | tf_op jit(solution)/shard_map/all_gather | solution.py:427
  75.9 14.4 %all-to-all-start.2 = ((bf16[4,384,128]{2,1,0:T(8,128)(2,1)}), bf16[4,384,128]{2,1,0:T(8,128)(2,1)S(1)}, u32[]{:S(2)}, u32[]{:S(2)}) async-start(bf16[4,384,128]{2,1,0:T(8,128)(2,1)} %get-tuple-element.36), calls=%async_computation.2 | async-start | bytes 786432 | tf_op jit(solution)/shard_map/all_to_all | solution.py:413
  90.3 1.7 %copy-start = (bf16[9600,128]{1,0:T(8,128)(2,1)S(1)}, bf16[9600,128]{1,0:T(8,128)(2,1)}, u32[]{:S(2)}) copy-start(bf16[9600,128]{1,0:T(8,128)(2,1)} %all-gather.14.cloned.1.call-done.right_ref) | copy-start | bytes 7372804
  128.2 0.6 copy-start.4
Sparse Core Ops, SparseCore 0:
  35.7 46.6 all-gather.13

commit v7 on v6

--- a/solution.py
+++ b/solution.py
@@ -347,6 +347,30 @@
     return ((r & 7) * ZH + ((r >> 3) & 3)) * PANEL + (r >> 5) * BLK
 
 
+def near_kernel(lists, own_ref, left_ref, near_ref, right_ref, sum_ref, diag_ref):
+    for o in range(SLOTS):
+        part = slice(o * BLK, (o + 1) * BLK)
+        sum_ref[part, :] = jnp.zeros((BLK, BLK), F32)
+        code = lists[TERMS + o, 64]
+
+        @pl.when(code > 0)
+        def _():
+            tile = right_ref[tile_at(panel_start(code)), :]
+            diag_ref[...] = dot(tile, tile).astype(BF16)
+
+        for t in range(LEFTS):
+            code = lists[TERMS + o, 32 + t]
+            left = left_at(t, left_ref, own_ref)
+
+            @pl.when((code >= OWN) & (code < PLAIN))
+            def _():
+                sum_ref[part, :] += dot(left[...], near_ref[tile_at((code - OWN) * BLK), :])
+
+            @pl.when(code == PLAIN)
+            def _():
+                sum_ref[part, :] += dot(left[...], diag_ref[...])
+
+
 def square_kernel(lists, own_ref, left_ref, right_ref, out_ref, near_ref, acc_ref):
     for o in range(SLOTS):
         part = slice(o * BLK, (o + 1) * BLK)
@@ -361,12 +385,6 @@
 
         tile = acc_ref[...].astype(BF16)
         near_ref[part, :] = tile
-        code = lists[TERMS + o, 64]
-
-        @pl.when(code > 0)
-        def _():
-            tile = right_ref[tile_at(panel_start(code)), :]
-            near_ref[TILES + o * BLK : TILES + (o + 1) * BLK, :] = dot(tile, tile).astype(BF16)
 
     for z in range(ZH):
         for c in range(ZROOM):
@@ -387,10 +405,10 @@
                 send_ref[d, c * BLK : (c + 1) * BLK, :] = square_ref[tile_at((code - 1) * BLK), :]
 
 
-def cube_kernel(lists, blocks, own_ref, left_ref, near_ref, right_ref, out_ref, level_ref, acc_ref):
+def cube_kernel(lists, blocks, own_ref, left_ref, sum_ref, right_ref, out_ref, level_ref, acc_ref):
     for o in range(SLOTS):
         part = slice(o * BLK, (o + 1) * BLK)
-        acc_ref[...] = jnp.zeros((BLK, BLK), F32)
+        acc_ref[...] = sum_ref[part, :]
         for t in range(LEFTS):
             code = lists[TERMS + o, 32 + t]
             left = left_at(t, left_ref, own_ref)
@@ -398,11 +416,6 @@
             @pl.when((code > 0) & (code <= Y * ROOM))
             def _():
                 acc_ref[...] += dot(left[...], right_ref[tile_at((code - 1) * BLK), :])
-
-            @pl.when(code >= OWN)
-            def _():
-                start = jnp.where(code == PLAIN, TILES + o * BLK, (code - OWN) * BLK)
-                acc_ref[...] += dot(left[...], near_ref[tile_at(start), :])
 
         value = 1.5 * own_ref[part, :].astype(F32) - 0.5 * acc_ref[...]
         out_ref[:, part] = jnp.where(blocks[0, o] >= 0, value, 0.0).astype(BF16)
@@ -454,7 +467,7 @@
     )(blocks, known, adjacent, wanted, ranks)
     square, near = pl.pallas_call(
         square_kernel,
-        out_shape=(like(ZH, ZROOM * BLK, BLK), like(2 * TILES, BLK)),
+        out_shape=(like(ZH, ZROOM * BLK, BLK), like(TILES, BLK)),
         in_specs=[SMEM] + [VMEM] * 3, out_specs=(VMEM, VMEM),
         scratch_shapes=[pltpu.VMEM((BLK, BLK), F32)], compiler_params=PARAMS, name="square",
     )(lists, own, left, right)
@@ -464,12 +477,20 @@
         out_shape=like(Y, ROOM * BLK, BLK),
         in_specs=[SMEM, VMEM], out_specs=VMEM, compiler_params=PARAMS, name="send",
     )(lists, square)
+    sums = pl.pallas_call(
+        near_kernel,
+        out_shape=like(TILES, BLK, dtype=F32),
+        in_specs=[SMEM] + [VMEM] * 4, out_specs=VMEM,
+        scratch_shapes=[pltpu.VMEM((BLK, BLK), BF16)],
+        cost_estimate=pl.CostEstimate(flops=2_000_000_000, bytes_accessed=1_000_000, transcendentals=0),
+        compiler_params=PARAMS, name="near",
+    )(lists, own, left, near, right)
     result, level = pl.pallas_call(
         cube_kernel,
         out_shape=(like(*x.shape), like(1, dtype=jnp.int32)),
         in_specs=[SMEM, SMEM] + [VMEM] * 4, out_specs=(VMEM, SMEM),
         scratch_shapes=[pltpu.VMEM((BLK, BLK), F32)], compiler_params=PARAMS, name="cube",
-    )(lists, blocks, own, left, near, swap(send, "y").reshape(Y * ROOM * BLK, BLK))
+    )(lists, blocks, own, left, sums, swap(send, "y").reshape(Y * ROOM * BLK, BLK))
     result, level, x, blocks = lax.optimization_barrier((result, level, x, blocks))
     return lax.cond(level[0] > 0, lambda: general(x, blocks), lambda: result)
 

time: 136 us -> 137 us (level)
  blocking collectives: 94.1 us -> 77.4 us
  waiting for transfers between devices: 5.49 us -> 15.9 us
  starting transfers between devices: 3.48 us -> 6.97 us
  Pallas kernels: 15.3 us -> 17.4 us
  local copies, waits for them, and re-layouts: 2.36 us -> 4.05 us
    all_to_all x4 -> x3, blocking collectives: 80.5 us -> 63.9 us  [swap(): return lax.all_to_all(value, axes, 0, 0, tiled=True)]
    all_to_all x1 -> x2, waiting for transfers between devices: 5.47 us -> 15.9 us  [swap(): return lax.all_to_all(value, axes, 0, 0, tiled=True)]
    all_to_all x1 -> x2, starting transfers between devices: 3.47 us -> 6.96 us  [swap(): return lax.all_to_all(value, axes, 0, 0, tiled=True)]
    pallas_call x0 -> x1, Pallas kernels: none -> 1.82 us  [per_device(): pl.pallas_call(near_kernel, out_shape=like(TILES, BLK, dtype=F32), in_spe...]
    unnamed x8 -> x10, local copies, waits for them, and re-layouts: 2.34 us -> 4.03 us
  transfers between devices with their start and end apart: 2 -> 3, of which waited for: 1 -> 2; matrix products, arithmetic and copies ran while one was open for 1% -> 1% of each run, Pallas kernels for 7% -> 8%
where the time goes in v7:
time: 137 us
  blocking collectives  77.4 us (56%)
  Pallas kernels  17.4 us (13%)
  waiting for transfers between devices  15.9 us (12%)
  between operations  14.2 us (10%)
  starting transfers between devices  6.97 us (5%)
  local copies, waits for them, and re-layouts  4.05 us (3%)
    all_to_all x3, blocking collectives, swap(): return lax.all_to_all(value, axes, 0, 0, tiled=True)  63.9 us
    all_to_all x2, waiting for transfers between devices, swap(): return lax.all_to_all(value, axes, 0, 0, tiled=True)  15.9 us
    all_gather x1, blocking collectives, per_device(): lax.all_gather(jnp.concatenate([own, heads], axis=0), ('x', 'c'), axis=0)  13.5 us
    all_to_all x2, starting transfers between devices, swap(): return lax.all_to_all(value, axes, 0, 0, tiled=True)  6.96 us
    pallas_call x1, Pallas kernels, per_device(): pl.pallas_call(term_kernel, out_shape=like(TERMS + 8, 128, dtype=jnp.int3...  5.54 us
    unnamed x10, local copies, waits for them, and re-layouts  4.03 us
    pallas_call x1, Pallas kernels, per_device(): pl.pallas_call(left_kernel, out_shape=(like(ZL, TILES, BLK), like(128, 12...  3.94 us
  transfers between devices with their start and end apart: 3, of which 2 were waited for; matrix products, arithmetic and copies ran while one was open for 1% of the time, Pallas kernels for 8%

profile of v7, /device:TPU:6, one launch (start us, length us, event | category | flops | bytes accessed | tf_op | source)
XLA Modules:
  0.0 136.9 jit_solution(2827176583311184222)
XLA Ops:
  6.5 0.0 all-gather.14.cloned.1.call-start
  6.5 1.0 pack.1
  7.5 28.0 %all_to_all.26 = bf16[3,400,128]{2,1,0:T(8,128)(2,1)} all-to-all(bf16[3,400,128]{2,1,0:T(8,128)(2,1)S(1)} %get-tuple-element.31), channel_id=1, replica_groups=mesh['zh'=3,'y'=8,'zl'=4,'x'=4,'c'=2] {'zh'}, dimensions={0} | all-to-all | bytes 614400 | tf_op jit(solution)/shard_map/all_to_all | solution.py:426
  35.5 0.0 all-gather.14.cloned.1.call-update
  35.5 0.7 slice_reduce_fusion.3
  36.3 13.5 %all-gather.second_ref = bf16[3200,128]{1,0:T(8,128)(2,1)S(1)} all-gather(bf16[400,128]{1,0:T(8,128)(2,1)S(1)} %pad_maximum_fusion), channel_id=2, replica_groups=mesh['zh'=3,'y'=8,'zl'=4,'x'=4,'c'=2] {'x','c'}, dimensions={0}, use_global_device_ids=true | all-gather | bytes 921600 | tf_op jit(solution)/shard_map/all_gather | solution.py:442
  49.8 22.0 %all_to_all.27 = bf16[32,16,128]{2,1,0:T(8,128)(2,1)S(1)} all-to-all(bf16[32,16,128]{2,1,0:T(8,128)(2,1)S(1)} %broadcast_in_dim.43), channel_id=1, replica_groups=mesh['zh'=3,'y'=8,'zl'=4,'x'=4,'c'=2] {'y','zl'}, dimensions={0} | all-to-all | bytes 262144 | tf_op jit(solution)/shard_map/all_to_all | solution.py:426
  71.9 3.9 %left.1 = (bf16[4,384,128]{2,1,0:T(8,128)(2,1)}, f32[128,128]{1,0:T(8,128)S(1)}, bf16[384,384]{1,0:T(8,128)(2,1)S(1)}, f32[32,128]{1,0:T(8,128)S(1)}, f32[32,128]{1,0:T(8,128)S(1)}) custom-call(bf16[8,64,128]{2,1,0:T(8,128)(2,1)S(1)} %bitcast.93, bf16[3200,128]{1,0:T(8,128)(2,1)S(1)} %all-gather.second_ref), custom_call_target="tpu_custom_call" | custom-call | tf_op jit(solution)/shard_map/left/pallas_call | solution.py:446
  75.8 3.5 %all-to-all-start.2 = ((bf16[4,384,128]{2,1,0:T(8,128)(2,1)}), bf16[4,384,128]{2,1,0:T(8,128)(2,1)S(1)}, u32[]{:S(2)}, u32[]{:S(2)}) async-start(bf16[4,384,128]{2,1,0:T(8,128)(2,1)} %get-tuple-element.36), calls=%async_computation.2 | async-start | bytes 786432 | tf_op jit(solution)/shard_map/all_to_all | solution.py:426
  79.3 0.0 copy-start.4
  79.3 0.0 copy-start.3
  79.3 5.5 %term.1.lists = s32[24,128]{1,0:T(8,128)S(1)} custom-call(s32[2,3]{1,0:T(2,128)} %blocks.5, f32[128,128]{1,0:T(8,128)S(1)} %get-tuple-element.32.gij_ref, bf16[384,384]{1,0:T(8,128)(2,1)S(1)} %get-tuple-element.33.adj_ref, f32[32,128]{1,0:T(8,128)S(1)} %get-tuple-element.34.dl_ref, f32[32,128]{1,0:T(8,128)S(1)} %get-tuple-element.35.rl_ref), custom_call_target="tpu_custom_call" | custom-call | flops 2000000000 | bytes 1000000 | tf_op jit(solution)/shard_map/term/pallas_call | solution.py:460
  84.9 5.3 %all-to-all-done.2 = bf16[4,384,128]{2,1,0:T(8,128)(2,1)S(1)} async-done(((bf16[4,384,128]{2,1,0:T(8,128)(2,1)}), bf16[4,384,128]{2,1,0:T(8,128)(2,1)S(1)}, u32[]{:S(2)}, u32[]{:S(2)}) %all-to-all-start.2) | async-done | bytes 393248 | tf_op jit(solution)/shard_map/all_to_all | solution.py:426
  90.2 0.0 all-gather.14.cloned.1.call-done.right_ref
  90.2 0.0 copy-start
  90.2 1.7 %copy-done = bf16[9600,128]{1,0:T(8,128)(2,1)S(1)} copy-done((bf16[9600,128]{1,0:T(8,128)(2,1)S(1)}, bf16[9600,128]{1,0:T(8,128)(2,1)}, u32[]{:S(2)}) %copy-start) | copy-done | bytes 2457624
  91.9 1.7 %square.1 = (bf16[3,256,128]{2,1,0:T(8,128)(2,1)S(1)}, bf16[384,128]{1,0:T(8,128)(2,1)S(1)}) custom-call(s32[24,128]{1,0:T(8,128)S(1)} %term.1.lists, bf16[384,128]{1,0:T(8,128)(2,1)S(1)} %get-tuple-element.30.own_ref, bf16[1536,128]{1,0:T(8,128)(2,1)S(1)} %bitcast.87, bf16[9600,128]{1,0:T(8,128)(2,1)S(1)} %copy-done), custom_call_target="tpu_custom_call" | custom-call | tf_op jit(solution)/shard_map/square/pallas_call | solution.py:468
  93.6 13.9 %all_to_all.28 = bf16[3,256,128]{2,1,0:T(8,128)(2,1)S(1)} all-to-all(bf16[3,256,128]{2,1,0:T(8,128)(2,1)S(1)} %get-tuple-element.38), channel_id=1, replica_groups=mesh['zh'=3,'y'=8,'zl'=4,'x'=4,'c'=2] {'zh'}, dimensions={0} | all-to-all | bytes 393216 | tf_op jit(solution)/shard_map/all_to_all | solution.py:426
  107.5 1.7 %send.1 = bf16[8,256,128]{2,1,0:T(8,128)(2,1)} custom-call(s32[24,128]{1,0:T(8,128)S(1)} %term.1.lists, bf16[768,128]{1,0:T(8,128)(2,1)S(1)} %bitcast.92), custom_call_target="tpu_custom_call" | custom-call | tf_op jit(solution)/shard_map/send/pallas_call | solution.py:475
  109.2 3.5 %all-to-all-start.4 = ((bf16[8,256,128]{2,1,0:T(8,128)(2,1)}), bf16[8,256,128]{2,1,0:T(8,128)(2,1)S(1)}, u32[]{:S(2)}, u32[]{:S(2)}) async-start(bf16[8,256,128]{2,1,0:T(8,128)(2,1)} %send.1), calls=%async_computation.4 | async-start | bytes 1048576 | tf_op jit(solution)/shard_map/all_to_all | solution.py:426
  112.7 0.0 copy-start.1
  112.7 1.7 %copy-done.1 = bf16[9600,128]{1,0:T(8,128)(2,1)S(1)} copy-done((bf16[9600,128]{1,0:T(8,128)(2,1)S(1)}, bf16[9600,128]{1,0:T(8,128)(2,1)}, u32[]{:S(2)}) %copy-start.1) | copy-done | bytes 2457624
  114.3 1.8 %near.1.sum_ref = f32[384,128]{1,0:T(8,128)S(1)} custom-call(s32[24,128]{1,0:T(8,128)S(1)} %term.1.lists, bf16[384,128]{1,0:T(8,128)(2,1)S(1)} %get-tuple-element.30.own_ref, bf16[1536,128]{1,0:T(8,128)(2,1)S(1)} %bitcast.88, bf16[384,128]{1,0:T(8,128)(2,1)S(1)} %get-tuple-element.37.near_ref, bf16[9600,128]{1,0:T(8,128)(2,1)S(1)} %copy-done.1), custom_call_target="tpu_custom_call" | custom-call | flops 2000000000 | bytes 1000000 | tf_op jit(solution)/shard_map/near/pallas_call | solution.py:480
  116.2 10.6 %all-to-all-done.4 = bf16[8,256,128]{2,1,0:T(8,128)(2,1)S(1)} async-done(((bf16[8,256,128]{2,1,0:T(8,128)(2,1)}), bf16[8,256,128]{2,1,0:T(8,128)(2,1)S(1)}, u32[]{:S(2)}, u32[]{:S(2)}) %all-to-all-start.4) | async-done | bytes 524320 | tf_op jit(solution)/shard_map/all_to_all | solution.py:426
  126.8 0.0 copy-done.4
  126.8 1.7 %cube.1 = (bf16[128,384]{1,0:T(8,128)(2,1)S(1)}, s32[1]{0:T(128)}) custom-call(s32[24,128]{1,0:T(8,128)S(1)} %term.1.lists, s32[2,3]{1,0:T(2,128)S(1)} %copy-done.4, bf16[384,128]{1,0:T(8,128)(2,1)S(1)} %get-tuple-element.30.own_ref, bf16[1536,128]{1,0:T(8,128)(2,1)S(1)} %bitcast.89, f32[384,128]{1,0:T(8,128)S(1)} %near.1.sum_ref, bf16[2048,128]{1,0:T(8,128)(2,1)S(1)} %bitcast.91), custom_call_target="tpu_custom_call" | custom-call | tf_op jit(solution)/shard_map/cube/pallas_call | solution.py:488
  129.1 0.0 copy-done.3
  129.1 0.2 conditional.1
  129.4 0.0 copy-start.5
  129.4 0.6 copy-done.5
  (3 shorter events, 0.0 us)
Async XLA Ops:
  6.5 83.7 %all-gather.14.cloned.1.call-start = ((), (), s32[]{:S(2)}) async-start(), calls=%async_computation.8 | async-start | bytes 2764800 | tf_op jit(solution)/shard_map/all_gather | solution.py:440
  75.8 14.4 %all-to-all-start.2 = ((bf16[4,384,128]{2,1,0:T(8,128)(2,1)}), bf16[4,384,128]{2,1,0:T(8,128)(2,1)S(1)}, u32[]{:S(2)}, u32[]{:S(2)}) async-start(bf16[4,384,128]{2,1,0:T(8,128)(2,1)} %get-tuple-element.36), calls=%async_computation.2 | async-start | bytes 786432 | tf_op jit(solution)/shard_map/all_to_all | solution.py:426
  79.3 47.5 %copy-start.4 = (s32[2,3]{1,0:T(2,128)S(1)}, s32[2,3]{1,0:T(2,128)}, u32[]{:S(2)}) copy-start(s32[2,3]{1,0:T(2,128)} %blocks.5) | copy-start | bytes 76
  79.3 49.8 %copy-start.3 = (bf16[128,384]{1,0:T(8,128)(2,1)S(1)}, bf16[128,384]{1,0:T(8,128)(2,1)}, u32[]{:S(2)}) copy-start(bf16[128,384]{1,0:T(8,128)(2,1)} %x_ref.1) | copy-start | bytes 294916
  90.2 1.7 %copy-start = (bf16[9600,128]{1,0:T(8,128)(2,1)S(1)}, bf16[9600,128]{1,0:T(8,128)(2,1)}, u32[]{:S(2)}) copy-start(bf16[9600,128]{1,0:T(8,128)(2,1)} %all-gather.14.cloned.1.call-done.right_ref) | copy-start | bytes 7372804
  109.2 17.6 %all-to-all-start.4 = ((bf16[8,256,128]{2,1,0:T(8,128)(2,1)}), bf16[8,256,128]{2,1,0:T(8,128)(2,1)S(1)}, u32[]{:S(2)}, u32[]{:S(2)}) async-start(bf16[8,256,128]{2,1,0:T(8,128)(2,1)} %send.1), calls=%async_computation.4 | async-start | bytes 1048576 | tf_op jit(solution)/shard_map/all_to_all | solution.py:426
  112.7 1.7 %copy-start.1 = (bf16[9600,128]{1,0:T(8,128)(2,1)S(1)}, bf16[9600,128]{1,0:T(8,128)(2,1)}, u32[]{:S(2)}) copy-start(bf16[9600,128]{1,0:T(8,128)(2,1)} %all-gather.14.cloned.1.call-done.right_ref) | copy-start | bytes 7372804
  129.4 0.6 copy-start.5
Sparse Core Ops, SparseCore 0:
  35.6 46.6 all-gather.13

commit v8 on v6

--- a/solution.py
+++ b/solution.py
@@ -14,6 +14,7 @@
 TILES = SLOTS * BLK
 HEAD = 16
 PANEL = TILES + HEAD
+SECOND = TILES + ZH * HEAD
 SLOTS_ROW = XC * SLOTS
 LEFTS = ZL * SLOTS + SLOTS
 OWN, PLAIN = 128, 160
@@ -202,7 +203,7 @@
             def _():
                 k = code - 1
                 src_u = (k * 11) >> 5
-                start = pl.multiple_of(src_u * PANEL + (k - src_u * SLOTS) * BLK, 16)
+                start = pl.multiple_of(src_u * SECOND + (k - src_u * SLOTS) * BLK, 16)
                 zbuf_ref[d, c * BLK : (c + 1) * BLK, :] = second_ref[pl.ds(start, BLK), :]
 
 
@@ -425,9 +426,9 @@
     )(blocks, x)
     first = swap(first, "zh")
     right = lax.all_gather(first.reshape(ZH * PANEL, BLK), "y", axis=0, tiled=True)
-    heads = jnp.sum(first[:, TILES:].astype(F32), axis=0).astype(BF16)
+    heads = first[:, TILES:].reshape(ZH * HEAD, 128)
     second = lax.all_gather(jnp.concatenate([own, heads], axis=0), ("x", "c"), axis=0)
-    heads = jnp.sum(second[:, TILES:].astype(F32), axis=0).astype(BF16)
+    heads = jnp.sum(second[:, TILES:].reshape(XC * ZH, HEAD, 128).astype(F32), axis=0).astype(BF16)
     heads = jnp.broadcast_to(heads[None], (Y * ZL, HEAD, 128)).reshape(Y * ZL * HEAD, 128)
     heads = swap(heads, ("y", "zl")).reshape(Y, ZL * HEAD, 128)
     zbuf, known, adjacent, wanted, ranks = pl.pallas_call(
@@ -442,7 +443,7 @@
             pltpu.VMEM((8, 128), jnp.int32), pltpu.SMEM((8, 128), jnp.int32), pltpu.SemaphoreType.DMA,
         ],
         compiler_params=PARAMS, name="left",
-    )(heads, second.reshape(XC * PANEL, BLK))
+    )(heads, second.reshape(XC * SECOND, BLK))
     left = swap(zbuf, "zl").reshape(ZL * TILES, BLK)
     lists = pl.pallas_call(
         term_kernel,

time: 136 us -> 136 us (level)
  no operation moved by 1% of the time
where the time goes in v8:
time: 136 us
  blocking collectives  94.6 us (70%)
  Pallas kernels  14.4 us (11%)
  between operations  14.1 us (10%)
  waiting for transfers between devices  5.84 us (4%)
  starting transfers between devices  3.48 us (3%)
  local copies, waits for them, and re-layouts  3.08 us (2%)
    all_to_all x4, blocking collectives, swap(): return lax.all_to_all(value, axes, 0, 0, tiled=True)  81 us
    all_gather x1, blocking collectives, per_device(): lax.all_gather(jnp.concatenate([own, heads], axis=0), ('x', 'c'), axis=0)  13.6 us
    all_to_all x1, waiting for transfers between devices, swap(): return lax.all_to_all(value, axes, 0, 0, tiled=True)  5.82 us
    pallas_call x1, Pallas kernels, per_device(): pl.pallas_call(term_kernel, out_shape=like(TERMS + 8, 128, dtype=jnp.int3...  5.41 us
    pallas_call x1, Pallas kernels, per_device(): pl.pallas_call(left_kernel, out_shape=(like(ZL, TILES, BLK), like(128, 12...  3.96 us
    all_to_all x1, starting transfers between devices, swap(): return lax.all_to_all(value, axes, 0, 0, tiled=True)  3.47 us
  transfers between devices with their start and end apart: 2, of which 1 were waited for; matrix products, arithmetic and copies ran while one was open for 1% of the time, Pallas kernels for 7%

profile of v8, /device:TPU:6, one launch (start us, length us, event | category | flops | bytes accessed | tf_op | source)
XLA Modules:
  0.0 135.8 jit_solution(6318622203326104040)
XLA Ops:
  6.5 0.0 copy-start.3
  6.5 0.0 copy-start.2
  6.5 0.0 all-gather.14.cloned.1.call-start
  6.5 1.0 pack.1
  7.6 28.0 %all_to_all.26 = bf16[3,400,128]{2,1,0:T(8,128)(2,1)} all-to-all(bf16[3,400,128]{2,1,0:T(8,128)(2,1)S(1)} %get-tuple-element.31), channel_id=1, replica_groups=mesh['zh'=3,'y'=8,'zl'=4,'x'=4,'c'=2] {'zh'}, dimensions={0} | all-to-all | bytes 614400 | tf_op jit(solution)/shard_map/all_to_all | solution.py:414
  35.6 0.0 all-gather.14.cloned.1.call-update
  35.6 0.7 slice.39
  36.3 13.6 %all-gather.second_ref = bf16[3456,128]{1,0:T(8,128)(2,1)S(1)} all-gather(bf16[432,128]{1,0:T(8,128)(2,1)S(1)} %pad_maximum_fusion), channel_id=2, replica_groups=mesh['zh'=3,'y'=8,'zl'=4,'x'=4,'c'=2] {'x','c'}, dimensions={0}, use_global_device_ids=true | all-gather | bytes 995328 | tf_op jit(solution)/shard_map/all_gather | solution.py:430
  50.0 22.0 %all_to_all.27 = bf16[32,16,128]{2,1,0:T(8,128)(2,1)S(1)} all-to-all(bf16[32,16,128]{2,1,0:T(8,128)(2,1)S(1)} %broadcast_in_dim.43), channel_id=1, replica_groups=mesh['zh'=3,'y'=8,'zl'=4,'x'=4,'c'=2] {'y','zl'}, dimensions={0} | all-to-all | bytes 262144 | tf_op jit(solution)/shard_map/all_to_all | solution.py:414
  72.0 4.0 %left.1 = (bf16[4,384,128]{2,1,0:T(8,128)(2,1)}, f32[128,128]{1,0:T(8,128)S(1)}, bf16[384,384]{1,0:T(8,128)(2,1)S(1)}, f32[32,128]{1,0:T(8,128)S(1)}, f32[32,128]{1,0:T(8,128)S(1)}) custom-call(bf16[8,64,128]{2,1,0:T(8,128)(2,1)S(1)} %bitcast.94, bf16[3456,128]{1,0:T(8,128)(2,1)S(1)} %all-gather.second_ref), custom_call_target="tpu_custom_call" | custom-call | tf_op jit(solution)/shard_map/left/pallas_call | solution.py:434
  76.0 3.5 %all-to-all-start.2 = ((bf16[4,384,128]{2,1,0:T(8,128)(2,1)}), bf16[4,384,128]{2,1,0:T(8,128)(2,1)S(1)}, u32[]{:S(2)}, u32[]{:S(2)}) async-start(bf16[4,384,128]{2,1,0:T(8,128)(2,1)} %get-tuple-element.36), calls=%async_computation.2 | async-start | bytes 786432 | tf_op jit(solution)/shard_map/all_to_all | solution.py:414
  79.4 5.4 %term.1.lists = s32[24,128]{1,0:T(8,128)S(1)} custom-call(s32[2,3]{1,0:T(2,128)} %blocks.5, f32[128,128]{1,0:T(8,128)S(1)} %get-tuple-element.32.gij_ref, bf16[384,384]{1,0:T(8,128)(2,1)S(1)} %get-tuple-element.33.adj_ref, f32[32,128]{1,0:T(8,128)S(1)} %get-tuple-element.34.dl_ref, f32[32,128]{1,0:T(8,128)S(1)} %get-tuple-element.35.rl_ref), custom_call_target="tpu_custom_call" | custom-call | flops 2000000000 | bytes 1000000 | tf_op jit(solution)/shard_map/term/pallas_call | solution.py:448
  84.9 5.8 %all-to-all-done.2 = bf16[4,384,128]{2,1,0:T(8,128)(2,1)S(1)} async-done(((bf16[4,384,128]{2,1,0:T(8,128)(2,1)}), bf16[4,384,128]{2,1,0:T(8,128)(2,1)S(1)}, u32[]{:S(2)}, u32[]{:S(2)}) %all-to-all-start.2) | async-done | bytes 393248 | tf_op jit(solution)/shard_map/all_to_all | solution.py:414
  90.7 0.0 all-gather.14.cloned.1.call-done.right_ref
  90.7 0.0 copy-start
  90.7 1.7 %copy-done = bf16[9600,128]{1,0:T(8,128)(2,1)S(1)} copy-done((bf16[9600,128]{1,0:T(8,128)(2,1)S(1)}, bf16[9600,128]{1,0:T(8,128)(2,1)}, u32[]{:S(2)}) %copy-start) | copy-done | bytes 2457624
  92.4 1.2 square.1
  93.6 14.4 %all_to_all.28 = bf16[3,256,128]{2,1,0:T(8,128)(2,1)S(1)} all-to-all(bf16[3,256,128]{2,1,0:T(8,128)(2,1)S(1)} %get-tuple-element.38), channel_id=1, replica_groups=mesh['zh'=3,'y'=8,'zl'=4,'x'=4,'c'=2] {'zh'}, dimensions={0} | all-to-all | bytes 393216 | tf_op jit(solution)/shard_map/all_to_all | solution.py:414
  108.0 0.9 send.1
  108.9 16.6 %all_to_all.29 = bf16[8,256,128]{2,1,0:T(8,128)(2,1)S(1)} all-to-all(bf16[8,256,128]{2,1,0:T(8,128)(2,1)S(1)} %send.1), channel_id=1, replica_groups=mesh['zh'=3,'y'=8,'zl'=4,'x'=4,'c'=2] {'y'}, dimensions={0} | all-to-all | bytes 1048576 | tf_op jit(solution)/shard_map/all_to_all | solution.py:414
  125.5 0.0 copy-done.3
  125.5 1.9 %cube.1 = (bf16[128,384]{1,0:T(8,128)(2,1)S(1)}, s32[1]{0:T(128)}) custom-call(s32[24,128]{1,0:T(8,128)S(1)} %term.1.lists, s32[2,3]{1,0:T(2,128)S(1)} %copy-done.3, bf16[384,128]{1,0:T(8,128)(2,1)S(1)} %get-tuple-element.30.own_ref, bf16[1536,128]{1,0:T(8,128)(2,1)S(1)} %bitcast.91, bf16[768,128]{1,0:T(8,128)(2,1)S(1)} %get-tuple-element.37.near_ref, ...), custom_call_target="tpu_custom_call" | custom-call | tf_op jit(solution)/shard_map/cube/pallas_call | solution.py:468
  128.1 0.0 copy-done.2
  128.1 0.2 conditional.1
  128.3 0.0 copy-start.4
  128.3 0.6 copy-done.4
  (4 shorter events, 0.1 us)
Async XLA Ops:
  6.5 119.0 %copy-start.3 = (s32[2,3]{1,0:T(2,128)S(1)}, s32[2,3]{1,0:T(2,128)}, u32[]{:S(2)}) copy-start(s32[2,3]{1,0:T(2,128)} %blocks.5) | copy-start | bytes 76
  6.5 121.5 %copy-start.2 = (bf16[128,384]{1,0:T(8,128)(2,1)S(1)}, bf16[128,384]{1,0:T(8,128)(2,1)}, u32[]{:S(2)}) copy-start(bf16[128,384]{1,0:T(8,128)(2,1)} %x_ref.1) | copy-start | bytes 294916
  6.5 84.1 %all-gather.14.cloned.1.call-start = ((), (), s32[]{:S(2)}) async-start(), calls=%async_computation.8 | async-start | bytes 2764800 | tf_op jit(solution)/shard_map/all_gather | solution.py:428
  76.0 14.7 %all-to-all-start.2 = ((bf16[4,384,128]{2,1,0:T(8,128)(2,1)}), bf16[4,384,128]{2,1,0:T(8,128)(2,1)S(1)}, u32[]{:S(2)}, u32[]{:S(2)}) async-start(bf16[4,384,128]{2,1,0:T(8,128)(2,1)} %get-tuple-element.36), calls=%async_computation.2 | async-start | bytes 786432 | tf_op jit(solution)/shard_map/all_to_all | solution.py:414
  90.7 1.7 %copy-start = (bf16[9600,128]{1,0:T(8,128)(2,1)S(1)}, bf16[9600,128]{1,0:T(8,128)(2,1)}, u32[]{:S(2)}) copy-start(bf16[9600,128]{1,0:T(8,128)(2,1)} %all-gather.14.cloned.1.call-done.right_ref) | copy-start | bytes 7372804
  128.3 0.6 copy-start.4
Sparse Core Ops, SparseCore 0:
  35.7 46.6 all-gather.13
